TPU v7x, 256 devices: a whole 4x4x8 slice. The times are simulated.
256 devices in a mesh: dp: 16 (over x, z_lo), factor: 16 (over z_hi, y, core).
Axes of the slice: x: 4, y: 4, z: 8 (z_hi: 2, z_lo: 4; z = z_hi * 4 + z_lo), core: 2. Of those that a mesh axis runs over, the one named last changes fastest.
Arguments:
- gradients: bfloat16 [16, 128, 512, 512], P('dp', 'factor'), as said below
- old_stats: float32 [16, 16, 512, 512], P('dp', 'factor'), as said below
- owner_table: int32 [16, 16], replicated, may hold values from 0 to 255, as said below
Outputs:
- new_stats: float32 [16, 16, 512, 512], P('dp', 'factor')
- roots: float32 [16, 16, 512, 512], P('dp', 'factor')
Inputs may be any that keep to these rules, and one draw needn't show every extreme that they name: `owner_table`: every owner f2 * 16 + d appears exactly once in the table. The 16 owners named by one column have distinct replica indices d, and for every factor index f2 the number of a column's owners with that factor index is 1. Each old_stats[d, f] is symmetric positive definite. `gradients`: gradient partials.
All inputs are finite; a program needn't handle non-finite values.
Results may differ from a plain program's by a relative error of at most 0.0003.
Values may be sent and summed in bfloat16 or wider, within the bound.
A program may use at most 128 MiB of HBM per device.

v0:
```python
import jax
import jax.numpy as jnp
from jax import lax
from jax.sharding import PartitionSpec as P

ITERS = 5


BETA = 0.9
HIGHEST = lax.Precision.HIGHEST


def inverse_root(stats):
    eye_matrix = jnp.eye(stats.shape[0], dtype=jnp.float32)
    scale = 2.5 / jnp.sqrt(jnp.sum(stats * stats) + 1e-06)
    moving = scale * stats
    root = eye_matrix
    for sweep in range(ITERS):
        factor = 1.25 * eye_matrix - 0.25 * moving
        root = jnp.dot(root, factor, precision=HIGHEST)
        square = jnp.dot(factor, factor, precision=HIGHEST)
        fourth = jnp.dot(square, square, precision=HIGHEST)
        moving = jnp.dot(fourth, moving, precision=HIGHEST)
    return jnp.sqrt(jnp.sqrt(scale)) * root


def local_partials(local_blocks, replicas):
    left_stats = jnp.einsum(
        "bik,bjk->bij", local_blocks, local_blocks, preferred_element_type=jnp.float32
    )
    right_stats = jnp.einsum(
        "bki,bkj->bij", local_blocks, local_blocks, preferred_element_type=jnp.float32
    )
    return jnp.stack((left_stats, right_stats), axis=1).reshape(
        replicas, local_blocks.shape[1], local_blocks.shape[2]
    )


def local(gradients, old_stats, owner_table):
    replicas = lax.axis_size("dp")
    owners = lax.axis_size("factor")
    quota = replicas // owners
    column = lax.axis_index("factor")
    slots = jnp.arange(replicas, dtype=jnp.int32)
    local_blocks = gradients[0]
    ranks = jnp.sum((owner_table[:, None, :] < owner_table[:, :, None]).astype(jnp.int32), axis=2)
    placed = (ranks[:, :, None] == slots[None, None, :]).astype(jnp.int32)
    sorted_matrix = jnp.sum(placed * slots[None, :, None], axis=1)
    sorted_owner = jnp.sum(placed * owner_table[:, :, None], axis=1)
    send_order = lax.dynamic_index_in_dim(sorted_matrix, column, 0, keepdims=False)
    arrived_owner = (
        lax.dynamic_slice_in_dim(sorted_owner, column * quota, quota, 1).reshape(-1)
        - column * replicas
    )
    pick = jnp.sum(jnp.where(arrived_owner[None, :] == slots[:, None], slots[None, :], 0), axis=1)
    partials = local_partials(local_blocks, replicas)
    outgoing = jnp.take(partials, send_order, axis=0)
    arrived = lax.all_to_all(outgoing, "factor", split_axis=0, concat_axis=0, tiled=True)
    ordered = jnp.take(arrived, pick, axis=0)
    summed = lax.psum_scatter(ordered, "dp", scatter_dimension=0, tiled=True)
    stats = BETA * old_stats[0, 0] + (1.0 - BETA) * summed[0]
    roots = inverse_root(stats)
    return (stats[None, None], roots[None, None])


def solution(mesh):
    placed = (P("dp", "factor", None, None), P("dp", "factor", None, None), P())
    return jax.shard_map(
        local,
        mesh=mesh,
        in_specs=placed,
        out_specs=(P("dp", "factor", None, None), P("dp", "factor", None, None)),
        check_vma=False,
    )
```

profile of v0, /device:TPU:1, one launch (start us, length us, event | category | flops | bytes accessed | tf_op | source)
XLA Modules:
  0.0 1002.2 jit_solution(4426125524605426716)
XLA Ops:
  7.2 0.0 copy-start.3
  7.2 9.1 fusion.7
  16.2 9.1 fusion.4
  25.3 0.0 copy-done.3
  25.3 0.4 convert_reduce_fusion
  25.7 0.2 select_reduce_fusion
  25.9 7.0 pad_maximum_fusion
  33.0 6.2 copy.11
  39.1 13.8 %gather_fusion = f32[16,512,512]{2,1,0:T(8,128)} fusion(f32[16,512,512]{2,1,0:T(8,128)} %bitcast.64, s32[1024]{0:T(1024)S(1)} %pad_clamp_fusion.1), kind=kCustom, calls=%fused_computation.clone | custom fusion | bytes 33554496 | tf_op jit(solution)/shard_map/jit(_take)/gather | solution.py:57
  53.0 11.9 %broadcast_select_fusion.1 = f32[16,512,512]{2,1,0:T(8,128)} fusion(f32[16,512,512]{2,1,0:T(8,128)} %gather_fusion, pred[16]{0:T(512)(128)(4,1)S(1)} %get-tuple-element.5), kind=kLoop, calls=%fused_computation.4 | loop fusion | flops 4194304 | bytes 33554448 | tf_op jit(solution)/shard_map/jit(_take)/select_n | solution.py:57
  64.9 12.6 %all-to-all-start = ((f32[16,512,512]{2,1,0:T(8,128)}), f32[16,512,512]{2,1,0:T(8,128)}, u32[]{:S(2)}, u32[]{:S(2)}) async-start(f32[16,512,512]{2,1,0:T(8,128)} %broadcast_select_fusion.1), calls=%async_computation | async-start | bytes 33554432 | tf_op jit(solution)/shard_map/all_to_all | solution.py:58
  77.5 0.0 reduce-scatter.2.cloned.1.call-start
  77.5 0.2 subtract_reduce_fusion
  77.7 0.1 select_reduce_fusion.2
  77.9 269.8 %all-to-all-done = f32[16,512,512]{2,1,0:T(8,128)} async-done(((f32[16,512,512]{2,1,0:T(8,128)}), f32[16,512,512]{2,1,0:T(8,128)}, u32[]{:S(2)}, u32[]{:S(2)}) %all-to-all-start) | async-done | bytes 16777248 | tf_op jit(solution)/shard_map/all_to_all | solution.py:58
  347.7 13.8 %gather_fusion.1 = f32[16,512,512]{2,1,0:T(8,128)} fusion(f32[16,512,512]{2,1,0:T(8,128)} %all-to-all-done, s32[1024]{0:T(1024)S(1)} %pad_clamp_fusion), kind=kCustom, calls=%fused_computation.1.clone | custom fusion | bytes 33554496 | tf_op jit(solution)/shard_map/jit(_take)/gather | solution.py:59
  361.5 12.3 %broadcast_select_fusion = f32[16,512,512]{2,1,0:T(8,128)} fusion(f32[16,512,512]{2,1,0:T(8,128)} %gather_fusion.1, pred[16]{0:T(512)(128)(4,1)S(1)} %compare_and_fusion), kind=kLoop, calls=%fused_computation.3 | loop fusion | flops 4194304 | bytes 33554448 | tf_op jit(solution)/shard_map/jit(_take)/select_n | solution.py:59
  373.8 0.0 copy-start
  373.8 0.0 reduce-scatter.2.cloned.1.call-update
  373.9 582.6 %reduce-scatter.2.cloned.1.call-done = f32[1,512,512]{2,1,0:T(8,128)} async-done(((f32[16,512,512]{2,1,0:T(8,128)}), f32[1,512,512]{2,1,0:T(8,128)}) %reduce-scatter.2.cloned.1.call-update) | async-done | bytes 1048592 | tf_op jit(solution)/shard_map/reduce_scatter | solution.py:60
  956.5 0.0 copy-done
  956.5 0.0 copy-start.1
  956.5 2.2 multiply_reduce_fusion
  959.5 1.5 bitcast_add_fusion.1
  960.9 0.0 copy-start.2
  961.0 2.0 fusion.12
  962.9 1.8 fusion.79
  964.8 3.2 fusion.19
  968.0 1.9 fusion.22
  969.9 0.0 copy-done.1
  969.9 1.3 fusion.11
  971.2 1.9 fusion.23
  973.1 1.8 fusion.80
  975.0 2.0 fusion.81
  977.0 1.9 fusion.24
  978.9 1.9 fusion.25
  980.8 1.8 fusion.82
  982.7 1.8 fusion.83
  984.5 0.0 copy-done.2
  984.6 1.9 fusion.26
  986.5 1.9 fusion.27
  988.4 2.1 fusion.84
  990.5 1.9 select_subtract_fusion
  992.3 2.8 fusion.10
  (5 shorter events, 0.0 us)
Async XLA Ops:
  7.2 18.1 %copy-start.3 = (s32[16,16]{1,0:T(8,128)S(1)}, s32[16,16]{1,0:T(8,128)}, u32[]{:S(2)}) copy-start(s32[16,16]{1,0:T(8,128)} %param.7) | copy-start | bytes 3076
  64.9 282.8 %all-to-all-start = ((f32[16,512,512]{2,1,0:T(8,128)}), f32[16,512,512]{2,1,0:T(8,128)}, u32[]{:S(2)}, u32[]{:S(2)}) async-start(f32[16,512,512]{2,1,0:T(8,128)} %broadcast_select_fusion.1), calls=%async_computation | async-start | bytes 33554432 | tf_op jit(solution)/shard_map/all_to_all | solution.py:58
  77.5 879.0 %reduce-scatter.2.cloned.1.call-start = ((), (), s32[]{:S(2)}) async-start(), calls=%async_computation.2 | async-start | bytes 17825792 | tf_op jit(solution)/shard_map/reduce_scatter | solution.py:60
  373.8 582.7 %copy-start = (f32[1,1,512,512]{3,2,1,0:T(8,128)S(1)}, f32[1,1,512,512]{3,2,1,0:T(8,128)}, u32[]{:S(2)}) copy-start(f32[1,1,512,512]{3,2,1,0:T(8,128)} %param.6) | copy-start | bytes 3145732
  956.5 13.4 %copy-start.1 = (f32[1,512,512]{2,1,0:T(8,128)S(1)}, f32[1,512,512]{2,1,0:T(8,128)}, u32[]{:S(2)}) copy-start(f32[1,512,512]{2,1,0:T(8,128)} %reduce-scatter.2.cloned.1.call-done) | copy-start | bytes 3145732
  960.9 23.6 %copy-start.2 = (f32[1,1,512,512]{3,2,1,0:T(8,128)}, f32[1,1,512,512]{3,2,1,0:T(8,128)S(1)}, u32[]{:S(2)}) copy-start(f32[1,1,512,512]{3,2,1,0:T(8,128)S(1)} %bitcast_add_fusion.1) | copy-start | bytes 3145732
Sparse Core Ops, SparseCore 0:
  374.0 582.4 reduce-scatter.1
where the time goes:
time: 1010 us; the launch traced here: 1000 us
  waiting for transfers between devices  852 us (84%)
  matrix products  52.2 us (5%)
  other arithmetic  35.8 us (4%)
  local copies, waits for them, and re-layouts  33.9 us (3%)
  between operations  15.3 us (2%)
  starting transfers between devices  12.7 us (1%)
    reduce_scatter x1, waiting for transfers between devices, local(): summed = lax.psum_scatter(ordered, 'dp', scatter_dimension=0, tiled=True)  583 us
    all_to_all x1, waiting for transfers between devices, local(): lax.all_to_all(outgoing, 'factor', split_axis=0, concat_axis=0, tiled=True)  270 us
  transfers between devices with their start and end apart: 2, of which 2 were waited for; matrix products, arithmetic and copies ran while one was open for 0% of the time, Pallas kernels for 0%

commit v1 on v0

v1 whole, which is shorter than its diff:
```python
import jax
import jax.numpy as jnp
from jax import lax
from jax.experimental import pallas as pl
from jax.experimental.pallas import tpu as pltpu
from jax.sharding import PartitionSpec as P

ITERS = 5
BETA = 0.9
B = 512
T = 128
MESH = pl.DeviceIdType.MESH
TILES = ((0, 0), (0, 1), (1, 1), (0, 2), (0, 3), (1, 2), (1, 3), (2, 2), (2, 3), (3, 3))
NT = len(TILES)
QUADS = ((0, 0), (0, 1), (1, 1))


def route(items_ref, columns_ref, grads, out, xg, part, r1, r2, xt, fs, fr, ds, dr,
          own_sem, xs, xr, zs, zr, ts, tr, as_, ar, bs, br):
    d = lax.axis_index("dp")
    f = lax.axis_index("factor")
    x, zl = d // 4, d % 4
    zh = f // 8
    q = zl + zh * (3 - 2 * zl)
    b0, b1 = q % 2, q // 2
    home = b0 * 8 + b1 * 4

    def dp_at(x_, q_, zh_):
        return x_ * 4 + q_ + zh_ * (3 - 2 * q_)

    def x_peer(k):
        return {"dp": dp_at((x + k) % 4, q, zh), "factor": f}

    def z_peer(step):
        flip = q + 1 - 2 * b0 if step == 0 else q + 2 - 4 * b1
        return {"dp": dp_at(x, flip, zh), "factor": f}

    def f_peer(g):
        return {"dp": dp_at(x, q, g // 8), "factor": g}

    def d_peer(e):
        return {"dp": e, "factor": f}

    barrier = pltpu.get_barrier_semaphore()
    for k in range(1, 16):
        pl.semaphore_signal(barrier, inc=1, device_id=d_peer((d + k) % 16), device_id_type=MESH)
        pl.semaphore_signal(barrier, inc=1, device_id=f_peer((f + k) % 16), device_id_type=MESH)
    own = [pltpu.make_async_copy(grads.at[2 * x + c], xg.at[c, 0], own_sem.at[c]) for c in range(2)]
    for copy in own:
        copy.start()
    pl.semaphore_wait(barrier, 30)

    def x_copy(c, k):
        return pltpu.make_async_remote_copy(
            src_ref=grads.at[2 * ((x + k) % 4) + c], dst_ref=xg.at[c, k],
            send_sem=xs.at[c, k], recv_sem=xr.at[c, k], device_id=x_peer(k), device_id_type=MESH)

    def z_copy(c, step):
        if step == 0:
            src, dst = part.at[c, pl.ds((1 - b0) * 8, 8)], r1.at[c]
        else:
            src, dst = part.at[c, pl.ds(b0 * 8 + (1 - b1) * 4, 4)], r2.at[c]
        return pltpu.make_async_remote_copy(
            src_ref=src, dst_ref=dst, send_sem=zs.at[c, step], recv_sem=zr.at[c, step],
            device_id=z_peer(step), device_id_type=MESH)

    def t_copy(c, k):
        return pltpu.make_async_remote_copy(
            src_ref=part.at[c, home + (x + k) % 4], dst_ref=xt.at[pl.ds(4 * x + 2 * c, 2)],
            send_sem=ts.at[c, k], recv_sem=tr.at[c, k], device_id=x_peer(k), device_id_type=MESH)

    def a_copy(g):
        return pltpu.make_async_remote_copy(
            src_ref=fs.at[g], dst_ref=fr.at[f], send_sem=as_.at[g], recv_sem=ar.at[f],
            device_id=f_peer(g), device_id_type=MESH)

    def a_landed(g):
        return pltpu.make_async_remote_copy(
            src_ref=fs.at[g], dst_ref=fr.at[g], send_sem=as_.at[g], recv_sem=ar.at[g],
            device_id=f_peer(g), device_id_type=MESH)

    piece = home + x

    def b_copy(e):
        return pltpu.make_async_remote_copy(
            src_ref=ds.at[e], dst_ref=dr.at[piece], send_sem=bs.at[e], recv_sem=br.at[piece],
            device_id=d_peer(e), device_id_type=MESH)

    def b_landed(e):
        e_x, e_zl = e // 4, e % 4
        e_q = e_zl + zh * (3 - 2 * e_zl)
        e_piece = (e_q % 2) * 8 + (e_q // 2) * 4 + e_x
        return pltpu.make_async_remote_copy(
            src_ref=ds.at[e], dst_ref=dr.at[e_piece], send_sem=bs.at[e], recv_sem=br.at[e_piece],
            device_id=d_peer(e), device_id_type=MESH)

    def grams(c):
        for side in range(2):
            for row, col in QUADS:
                total = None
                for k in range(4):
                    if side == 0:
                        left = xg[c, k, row * 256:(row + 1) * 256, :]
                        right = xg[c, k, col * 256:(col + 1) * 256, :]
                        dims = (((1,), (1,)), ((), ()))
                    else:
                        left = xg[c, k, :, row * 256:(row + 1) * 256]
                        right = xg[c, k, :, col * 256:(col + 1) * 256]
                        dims = (((0,), (0,)), ((), ()))
                    term = lax.dot_general(left, right, dims, preferred_element_type=jnp.float32)
                    total = term if total is None else total + term
                for n, (i, j) in enumerate(TILES):
                    if i // 2 == row and j // 2 == col:
                        i0, j0 = (i % 2) * T, (j % 2) * T
                        part[c, :, side, n] = total[i0:i0 + T, j0:j0 + T].reshape(16, 8, T)

    def fold(c, step):
        if step == 0:
            part[c, pl.ds(b0 * 8, 8)] += r1[c]
        else:
            part[c, pl.ds(home, 4)] += r2[c]

    def spread(c):
        for k in (2, 1, 3):
            t_copy(c, k).start()
        xt[pl.ds(4 * x + 2 * c, 2)] = part[c, home + x]

    order = (2, 1, 3)
    for k in order:
        x_copy(0, k).start()
    for k in order:
        x_copy(0, k).wait_send()
    for k in order:
        x_copy(1, k).start()
    own[0].wait()
    for k in order:
        x_copy(0, k).wait_recv()
    grams(0)
    z_copy(0, 0).start()
    z_copy(0, 0).wait_recv()
    fold(0, 0)
    z_copy(0, 1).start()
    own[1].wait()
    for k in order:
        x_copy(1, k).wait_recv()
    grams(1)
    z_copy(1, 0).start()
    z_copy(0, 1).wait_recv()
    fold(0, 1)
    spread(0)
    z_copy(1, 0).wait_recv()
    fold(1, 0)
    z_copy(1, 1).start()
    z_copy(1, 1).wait_recv()
    fold(1, 1)
    spread(1)
    for c in range(2):
        for k in order:
            t_copy(c, k).wait_recv()

    for k in range(1, 16):
        g = (f + k) % 16
        fs[g] = xt[items_ref[g]]
        a_copy(g).start()
    fr[f] = xt[items_ref[f]]
    for k in range(1, 16):
        a_landed((f + k) % 16).wait_recv()
    for k in range(1, 16):
        e = (d + k) % 16
        ds[e] = fr[columns_ref[e]]
        b_copy(e).start()
    dr[piece] = fr[columns_ref[d]]
    for k in range(1, 16):
        b_landed((d + k) % 16).wait_recv()
    out[...] = dr[...]

    for k in order:
        x_copy(1, k).wait_send()
    for c in range(2):
        for step in range(2):
            z_copy(c, step).wait_send()
        for k in order:
            t_copy(c, k).wait_send()
    for k in range(1, 16):
        a_copy((f + k) % 16).wait_send()
        b_copy((d + k) % 16).wait_send()


def routed(items, columns, grads):
    tile = (NT, 8, T)
    return pl.pallas_call(
        route,
        out_shape=jax.ShapeDtypeStruct((16,) + tile, jnp.float32),
        in_specs=[
            pl.BlockSpec(memory_space=pltpu.SMEM),
            pl.BlockSpec(memory_space=pltpu.SMEM),
            pl.BlockSpec(memory_space=pl.ANY),
        ],
        out_specs=pl.BlockSpec(memory_space=pltpu.VMEM),
        scratch_shapes=[
            pltpu.VMEM((2, 4, B, B), jnp.bfloat16),
            pltpu.VMEM((2, 16, 2) + tile, jnp.float32),
            pltpu.VMEM((2, 8, 2) + tile, jnp.float32),
            pltpu.VMEM((2, 4, 2) + tile, jnp.float32),
            pltpu.VMEM((16,) + tile, jnp.float32),
            pltpu.VMEM((16,) + tile, jnp.float32),
            pltpu.VMEM((16,) + tile, jnp.float32),
            pltpu.VMEM((16,) + tile, jnp.float32),
            pltpu.VMEM((16,) + tile, jnp.float32),
            pltpu.SemaphoreType.DMA((2,)),
            pltpu.SemaphoreType.DMA((2, 4)),
            pltpu.SemaphoreType.DMA((2, 4)),
            pltpu.SemaphoreType.DMA((2, 2)),
            pltpu.SemaphoreType.DMA((2, 2)),
            pltpu.SemaphoreType.DMA((2, 4)),
            pltpu.SemaphoreType.DMA((2, 4)),
            pltpu.SemaphoreType.DMA((16,)),
            pltpu.SemaphoreType.DMA((16,)),
            pltpu.SemaphoreType.DMA((16,)),
            pltpu.SemaphoreType.DMA((16,)),
        ],
        compiler_params=pltpu.CompilerParams(
            collective_id=0, has_side_effects=True, vmem_limit_bytes=48 * 1024 * 1024
        ),
        cost_estimate=pl.CostEstimate(flops=4 * 10**9, bytes_accessed=8 * 10**6, transcendentals=0),
        name="route",
    )(items, columns, grads)


def split(a):
    high = a.astype(jnp.bfloat16)
    return high, (a - high.astype(jnp.float32)).astype(jnp.bfloat16)


def product(a, b):
    def dot(left, right):
        return jnp.dot(left, right, preferred_element_type=jnp.float32)

    return dot(a[0], b[0]) + (dot(a[0], b[1]) + dot(a[1], b[0]))


def newton(tri, old, stats, roots, moving, root):
    for n, (i, j) in enumerate(TILES):
        block = tri[:, n].reshape(T, T)
        rows, cols = slice(i * T, (i + 1) * T), slice(j * T, (j + 1) * T)
        stats[rows, cols] = BETA * old[rows, cols] + (1.0 - BETA) * block
        if i != j:
            stats[cols, rows] = BETA * old[cols, rows] + (1.0 - BETA) * block.T
    scale = 2.5 / jnp.sqrt(jnp.sum(stats[...] * stats[...], keepdims=True) + 1e-06)
    eye = (lax.broadcasted_iota(jnp.int32, (B, B), 0) == lax.broadcasted_iota(jnp.int32, (B, B), 1))

    def factor_of(m):
        return jnp.where(eye, 1.25, 0.0) - 0.25 * m

    def advance(factor, m):
        square = split(product(factor, factor))
        fourth = split(product(square, square))
        moving[...] = product(fourth, split(m))

    m = scale * stats[...]
    first = factor_of(m)
    root[...] = first
    advance(split(first), m)

    def sweep(_, carry):
        m = moving[...]
        factor = split(factor_of(m))
        root[...] = product(split(root[...]), factor)
        advance(factor, m)
        return carry

    lax.fori_loop(0, ITERS - 2, sweep, 0)
    last = product(split(root[...]), split(factor_of(moving[...])))
    roots[...] = jnp.sqrt(jnp.sqrt(scale)) * last


def finished(tri, old):
    whole = pl.BlockSpec(memory_space=pltpu.VMEM)
    return pl.pallas_call(
        newton,
        out_shape=(jax.ShapeDtypeStruct((B, B), jnp.float32),) * 2,
        in_specs=[whole, whole],
        out_specs=(whole, whole),
        scratch_shapes=[pltpu.VMEM((B, B), jnp.float32)] * 2,
        compiler_params=pltpu.CompilerParams(vmem_limit_bytes=48 * 1024 * 1024),
        cost_estimate=pl.CostEstimate(flops=13 * 10**9, bytes_accessed=4 * 10**6, transcendentals=0),
        name="newton",
    )(tri, old)


def local(gradients, old_stats, owner_table):
    f = lax.axis_index("factor")
    slots = jnp.arange(16, dtype=jnp.int32)
    mine = lax.dynamic_index_in_dim(owner_table, f, 0, keepdims=False)
    items = jnp.sum(jnp.where(mine[None, :] // 16 == slots[:, None], slots[None, :], 0), axis=1)
    wanted = (owner_table[None] == f * 16 + slots[:, None, None])
    columns = jnp.sum(jnp.where(wanted, slots[None, :, None], 0), axis=(1, 2))
    tri = routed(items, columns, gradients[0])
    stats, roots = finished(tri, old_stats[0, 0])
    return (stats[None, None], roots[None, None])


def solution(mesh):
    placed = (P("dp", "factor", None, None), P("dp", "factor", None, None), P())
    return jax.shard_map(
        local,
        mesh=mesh,
        in_specs=placed,
        out_specs=(P("dp", "factor", None, None), P("dp", "factor", None, None)),
        check_vma=False,
    )
```

time: 1010 us -> 147 us (0.15)
  waiting for transfers between devices: 852 us -> 0 us
  Pallas kernels: 0 us -> 141 us
  matrix products: 52.2 us -> 0 us
  other arithmetic: 35.8 us -> 1.96 us
  local copies, waits for them, and re-layouts: 33.9 us -> 2.19 us
  between operations: 15.3 us -> 0.66 us
  starting transfers between devices: 12.7 us -> 0 us
    reduce_scatter x1 -> x0, waiting for transfers between devices: 583 us -> none  [local(): summed = lax.psum_scatter(ordered, 'dp', scatter_dimension=0, tiled=True)]
    all_to_all x1 -> x0, waiting for transfers between devices: 270 us -> none  [local(): lax.all_to_all(outgoing, 'factor', split_axis=0, concat_axis=0, tiled=True)]
    pallas_call x0 -> x2, Pallas kernels: none -> 141 us  [the longest x1 125 us: routed(): pl.pallas_call(route, out_shape=jax.ShapeDtypeStruct((16,) + tile, jnp.fl...]
    dot_general x19 -> x0, matrix products: 52.2 us -> none  [the longest x5 9.83 us: inverse_root(): root = jnp.dot(root, factor, precision=HIGHEST)]
    gather x2 -> x0, local copies, waits for them, and re-layouts: 27.7 us -> none  [the longest x1 13.8 us: local(): outgoing = jnp.take(partials, send_order, axis=0)]
    select_n x3 -> x0, other arithmetic: 24.2 us -> none  [the longest x2 12.3 us: local(): ordered = jnp.take(arrived, pick, axis=0)]
    all_to_all x1 -> x0, starting transfers between devices: 12.6 us -> none  [local(): lax.all_to_all(outgoing, 'factor', split_axis=0, concat_axis=0, tiled=True)]
  transfers between devices with their start and end apart: 2 -> 0, of which waited for: 2 -> 0; matrix products, arithmetic and copies ran while one was open for 0% -> 0% of each run, Pallas kernels for 0% -> 0%
where the time goes in v1:
time: 147 us; the launch traced here: 146 us
  Pallas kernels  141 us (96%)
  local copies, waits for them, and re-layouts  2.19 us (1%)
  other arithmetic  1.96 us (1%)
    pallas_call x1, Pallas kernels, routed(): pl.pallas_call(route, out_shape=jax.ShapeDtypeStruct((16,) + tile, jnp.fl...  125 us
    pallas_call x1, Pallas kernels, finished(): pl.pallas_call(newton, out_shape=(jax.ShapeDtypeStruct((B, B), jnp.float3...  15.8 us

profile of v1, /device:TPU:1, one launch (start us, length us, event | category | flops | bytes accessed | tf_op | source)
XLA Modules:
  0.0 145.9 jit_solution(5883566025347529713)
XLA Ops:
  0.6 0.7 fusion
  1.3 0.1 select_reduce_fusion.1.items_ref
  1.5 1.1 select_reduce_fusion.columns_ref
  2.6 0.0 copy-start
  2.6 2.2 %copy-done = bf16[1,8,512,512]{3,2,1,0:T(8,128)(2,1)S(1)} copy-done((bf16[1,8,512,512]{3,2,1,0:T(8,128)(2,1)S(1)}, bf16[1,8,512,512]{3,2,1,0:T(8,128)(2,1)}, u32[]{:S(2)}) %copy-start) | copy-done | bytes 4194328
  4.8 0.0 copy-start.1
  4.8 125.2 %route.1.tri = f32[16,10,8,128]{3,2,1,0:T(8,128)S(1)} custom-call(s32[16]{0:T(128)S(1)} %select_reduce_fusion.1.items_ref, s32[16]{0:T(128)S(1)} %select_reduce_fusion.columns_ref, bf16[8,512,512]{2,1,0:T(8,128)(2,1)S(1)} %bitcast.6), custom_call_target="tpu_custom_call" | custom-call | flops 4000000000 | bytes 8000000 | tf_op jit(solution)/shard_map/route/pallas_call | solution.py:191
  130.0 0.0 copy-done.1
  130.0 15.8 %newton.1 = (f32[512,512]{1,0:T(8,128)}, f32[512,512]{1,0:T(8,128)}) custom-call(f32[16,10,8,128]{3,2,1,0:T(8,128)S(1)} %route.1.tri, f32[512,512]{1,0:T(8,128)S(1)} %bitcast.7), custom_call_target="tpu_custom_call" | custom-call | flops 12999999488 | bytes 4000000 | tf_op jit(solution)/shard_map/newton/pallas_call | solution.py:279
  (1 shorter events, 0.0 us)
Async XLA Ops:
  2.6 2.2 %copy-start = (bf16[1,8,512,512]{3,2,1,0:T(8,128)(2,1)S(1)}, bf16[1,8,512,512]{3,2,1,0:T(8,128)(2,1)}, u32[]{:S(2)}) copy-start(bf16[1,8,512,512]{3,2,1,0:T(8,128)(2,1)} %param.3) | copy-start | bytes 12582916
  4.8 125.2 %copy-start.1 = (f32[1,1,512,512]{3,2,1,0:T(8,128)S(1)}, f32[1,1,512,512]{3,2,1,0:T(8,128)}, u32[]{:S(2)}) copy-start(f32[1,1,512,512]{3,2,1,0:T(8,128)} %param.4) | copy-start | bytes 3145732

commit v2 on v1

v2 whole, which is shorter than its diff:
```python
import jax
import jax.numpy as jnp
from jax import lax
from jax.experimental import pallas as pl
from jax.experimental.pallas import tpu as pltpu
from jax.sharding import PartitionSpec as P

ITERS = 5
BETA = 0.9
B = 512
T = 128
MESH = pl.DeviceIdType.MESH
TILES = ((0, 1), (0, 2), (0, 3), (1, 2), (1, 3), (2, 3), (0, 0), (1, 1), (2, 2))
NT = len(TILES)
H = 256
QUADS = ((1, 1), (0, 0), (0, 1))


def low_left():
    rows = lax.broadcasted_iota(jnp.int32, (T, T), 0)
    cols = lax.broadcasted_iota(jnp.int32, (T, T), 1)
    return jnp.logical_and(rows >= T // 2, cols < T // 2)


def swapped(block):
    return jnp.concatenate([block[T // 2:], block[:T // 2]], axis=0)


def turned(block):
    return jnp.concatenate([block[:, T // 2:], block[:, :T // 2]], axis=1)


def route(table, grads, out, xg, part, r1, r2, xt, fs, fr, ds, dr, items, columns,
          own_sem, xs, xr, zs, zr, ts, tr, as_, ar, bs, br, turn):
    d = lax.axis_index("dp")
    f = lax.axis_index("factor")
    x, zl = d // 4, d % 4
    zh, core = f // 8, f % 2
    q = zl + zh * (3 - 2 * zl)
    b0, b1 = q % 2, q // 2
    home = b0 * 8 + b1 * 4
    piece = home + x

    def dp_at(x_, q_, zh_):
        return x_ * 4 + q_ + zh_ * (3 - 2 * q_)

    def x_peer(k):
        return {"dp": dp_at((x + k) % 4, q, zh), "factor": f}

    def z_peer(step):
        flip = q + 1 - 2 * b0 if step == 0 else q + 2 - 4 * b1
        return {"dp": dp_at(x, flip, zh), "factor": f}

    def f_peer(g):
        return {"dp": dp_at(x, q, g // 8), "factor": g}

    def d_peer(e):
        return {"dp": e, "factor": f}

    barrier = pltpu.get_barrier_semaphore()
    for k in range(1, 16):
        pl.semaphore_signal(barrier, inc=1, device_id=d_peer((d + k) % 16), device_id_type=MESH)
        pl.semaphore_signal(barrier, inc=1, device_id=f_peer((f + k) % 16), device_id_type=MESH)
    own = [pltpu.make_async_copy(grads.at[2 * x + c], xg.at[c, 0], own_sem.at[c]) for c in range(2)]
    for copy in own:
        copy.start()

    owners = [table[f, j] for j in range(16)]
    for g in range(16):
        pick = jnp.int32(0)
        for j in range(16):
            pick = jnp.where(lax.shift_right_logical(owners[j], 4) == g, j, pick)
        items[g] = pick

    def find_column(e, carry):
        def scan(c, found):
            for j in range(16):
                found = jnp.where(table[c, j] == f * 16 + e, c, found)
            return found
        columns[e] = lax.fori_loop(0, 16, scan, jnp.int32(0))
        return carry

    pl.semaphore_wait(barrier, 30)

    def x_copy(c, k):
        return pltpu.make_async_remote_copy(
            src_ref=grads.at[2 * ((x + k) % 4) + c], dst_ref=xg.at[c, k],
            send_sem=xs.at[c, k], recv_sem=xr.at[c, k], device_id=x_peer(k), device_id_type=MESH)

    def z_copy(c, side, step):
        if step == 0:
            src, dst = part.at[c, side, pl.ds((1 - b0) * 8, 8)], r1.at[c, side]
        else:
            src, dst = part.at[c, side, pl.ds(b0 * 8 + (1 - b1) * 4, 4)], r2.at[c, side]
        return pltpu.make_async_remote_copy(
            src_ref=src, dst_ref=dst, send_sem=zs.at[c, side, step], recv_sem=zr.at[c, side, step],
            device_id=z_peer(step), device_id_type=MESH)

    def t_copy(c, side, k):
        return pltpu.make_async_remote_copy(
            src_ref=part.at[c, side, home + (x + k) % 4], dst_ref=xt.at[4 * x + 2 * c + side],
            send_sem=ts.at[c, side, k], recv_sem=tr.at[c, side, k], device_id=x_peer(k), device_id_type=MESH)

    def a_copy(g):
        return pltpu.make_async_remote_copy(
            src_ref=fs.at[g], dst_ref=fr.at[f], send_sem=as_.at[g], recv_sem=ar.at[f],
            device_id=f_peer(g), device_id_type=MESH)

    def a_landed(g):
        return pltpu.make_async_remote_copy(
            src_ref=fs.at[g], dst_ref=fr.at[g], send_sem=as_.at[g], recv_sem=ar.at[g],
            device_id=f_peer(g), device_id_type=MESH)

    def b_copy(e):
        return pltpu.make_async_remote_copy(
            src_ref=ds.at[e], dst_ref=dr.at[piece], send_sem=bs.at[e], recv_sem=br.at[piece],
            device_id=d_peer(e), device_id_type=MESH)

    def b_landed(e):
        e_x, e_zl = e // 4, e % 4
        e_q = e_zl + zh * (3 - 2 * e_zl)
        e_piece = (e_q % 2) * 8 + (e_q // 2) * 4 + e_x
        return pltpu.make_async_remote_copy(
            src_ref=ds.at[e], dst_ref=dr.at[e_piece], send_sem=bs.at[e], recv_sem=br.at[e_piece],
            device_id=d_peer(e), device_id_type=MESH)

    def gram(c, side):
        corner = None
        corner_parts = ()
        for row, col in QUADS:
            total = None
            for k in range(4):
                if side == 0:
                    left = xg[c, k, row * H:(row + 1) * H, :]
                    right = xg[c, k, col * H:(col + 1) * H, :]
                    dims = (((1,), (1,)), ((), ()))
                else:
                    left = xg[c, k, :, row * H:(row + 1) * H]
                    right = xg[c, k, :, col * H:(col + 1) * H]
                    dims = (((0,), (0,)), ((), ()))
                term = lax.dot_general(left, right, dims, preferred_element_type=jnp.float32)
                total = term if total is None else total + term
            if corner is None:
                corner = total[T:, T:]
                shifted = swapped(corner)
                corner_parts = (shifted, turned(shifted), turned(corner))
            for n, (i, j) in enumerate(TILES):
                if i // 2 == row and j // 2 == col:
                    i0, j0 = (i % 2) * T, (j % 2) * T
                    block = total[i0:i0 + T, j0:j0 + T]
                    if i == j:
                        block = jnp.where(low_left(), corner_parts[i], block)
                    part[c, side, :, n] = block.reshape(16, 8, T)

    def fold(c, side, step):
        if step == 0:
            part[c, side, pl.ds(b0 * 8, 8)] += r1[c, side]
        else:
            part[c, side, pl.ds(home, 4)] += r2[c, side]

    def spread(c, side):
        for k in order:
            t_copy(c, side, k).start()
        xt[4 * x + 2 * c + side] = part[c, side, piece]

    order = (2, 1, 3)

    def send_x():
        for c in range(2):
            for k in order:
                x_copy(c, k).start()
            for k in order:
                x_copy(c, k).wait_send()

    @pl.when(core == 0)
    def _():
        send_x()
        pl.semaphore_signal(turn, inc=1, device_id={"dp": d, "factor": f + 1}, device_id_type=MESH)

    @pl.when(core == 1)
    def _():
        pl.semaphore_wait(turn, 1)
        send_x()

    lax.fori_loop(0, 16, find_column, 0)

    def arrive(c):
        own[c].wait()
        for k in order:
            x_copy(c, k).wait_recv()
        for side in range(2):
            gram(c, side)
            z_copy(c, side, 0).start()

    def halve(c):
        for side in range(2):
            z_copy(c, side, 0).wait_recv()
            fold(c, side, 0)
            z_copy(c, side, 1).start()

    def settle(c):
        for side in range(2):
            z_copy(c, side, 1).wait_recv()
            fold(c, side, 1)
            spread(c, side)

    arrive(0)
    halve(0)
    arrive(1)
    settle(0)
    halve(1)
    settle(1)
    for c in range(2):
        for side in range(2):
            for k in order:
                t_copy(c, side, k).wait_recv()

    for k in range(1, 16):
        g = (f + k) % 16
        fs[g] = xt[items[g]]
        a_copy(g).start()
    fr[f] = xt[items[f]]
    for k in range(1, 16):
        a_landed((f + k) % 16).wait_recv()
    for k in range(1, 16):
        e = (d + k) % 16
        ds[e] = fr[columns[e]]
        b_copy(e).start()
    dr[piece] = fr[columns[d]]
    for k in range(1, 16):
        b_landed((d + k) % 16).wait_recv()
    out[...] = dr[...]

    for c in range(2):
        for side in range(2):
            for step in range(2):
                z_copy(c, side, step).wait_send()
            for k in order:
                t_copy(c, side, k).wait_send()
    for k in range(1, 16):
        a_copy((f + k) % 16).wait_send()
        b_copy((d + k) % 16).wait_send()


def routed(table, grads):
    tile = (NT, 8, T)
    return pl.pallas_call(
        route,
        out_shape=jax.ShapeDtypeStruct((16,) + tile, jnp.float32),
        in_specs=[
            pl.BlockSpec(memory_space=pltpu.SMEM),
            pl.BlockSpec(memory_space=pltpu.HBM),
        ],
        out_specs=pl.BlockSpec(memory_space=pltpu.VMEM),
        scratch_shapes=[
            pltpu.VMEM((2, 4, B, B), jnp.bfloat16),
            pltpu.VMEM((2, 2, 16) + tile, jnp.float32),
            pltpu.VMEM((2, 2, 8) + tile, jnp.float32),
            pltpu.VMEM((2, 2, 4) + tile, jnp.float32),
            pltpu.VMEM((16,) + tile, jnp.float32),
            pltpu.VMEM((16,) + tile, jnp.float32),
            pltpu.VMEM((16,) + tile, jnp.float32),
            pltpu.VMEM((16,) + tile, jnp.float32),
            pltpu.VMEM((16,) + tile, jnp.float32),
            pltpu.SMEM((16,), jnp.int32),
            pltpu.SMEM((16,), jnp.int32),
            pltpu.SemaphoreType.DMA((2,)),
            pltpu.SemaphoreType.DMA((2, 4)),
            pltpu.SemaphoreType.DMA((2, 4)),
            pltpu.SemaphoreType.DMA((2, 2, 2)),
            pltpu.SemaphoreType.DMA((2, 2, 2)),
            pltpu.SemaphoreType.DMA((2, 2, 4)),
            pltpu.SemaphoreType.DMA((2, 2, 4)),
            pltpu.SemaphoreType.DMA((16,)),
            pltpu.SemaphoreType.DMA((16,)),
            pltpu.SemaphoreType.DMA((16,)),
            pltpu.SemaphoreType.DMA((16,)),
            pltpu.SemaphoreType.REGULAR,
        ],
        compiler_params=pltpu.CompilerParams(
            collective_id=0, has_side_effects=True, vmem_limit_bytes=60 * 1024 * 1024
        ),
        cost_estimate=pl.CostEstimate(flops=4 * 10**9, bytes_accessed=8 * 10**6, transcendentals=0),
        name="route",
    )(table, grads)


def split(a):
    high = a.astype(jnp.bfloat16)
    return high, (a - high.astype(jnp.float32)).astype(jnp.bfloat16)


def dot(left, right):
    return jnp.dot(left, right, preferred_element_type=jnp.float32)


def product(a, b):
    def quad(r, c):
        rows, cols = slice(r * H, (r + 1) * H), slice(c * H, (c + 1) * H)
        return dot(a[0][rows], b[0][:, cols]) + (dot(a[0][rows], b[1][:, cols]) + dot(a[1][rows], b[0][:, cols]))

    upper = quad(0, 1)
    top = jnp.concatenate([quad(0, 0), upper], axis=1)
    return jnp.concatenate([top, jnp.concatenate([upper.T, quad(1, 1)], axis=1)], axis=0)


def newton(tri, old, stats, roots, moving, root):
    def blend(i, j, block):
        rows, cols = slice(i * T, (i + 1) * T), slice(j * T, (j + 1) * T)
        stats[rows, cols] = BETA * old[rows, cols] + (1.0 - BETA) * block

    mask = low_left()
    kept = []
    for n, (i, j) in enumerate(TILES):
        block = tri[:, n].reshape(T, T)
        if i == j:
            kept.append(block)
            blend(i, i, jnp.where(mask, block.T, block))
        else:
            blend(i, j, block)
            blend(j, i, block.T)
    first, second, third = kept
    left = lax.broadcasted_iota(jnp.int32, (T // 2, T), 1) < T // 2
    top = jnp.where(left, first[T // 2:], turned(second[T // 2:]))
    corner = jnp.concatenate([top, turned(third[T // 2:])], axis=0)
    blend(3, 3, jnp.where(mask, corner.T, corner))

    scale = 2.5 / jnp.sqrt(jnp.sum(stats[...] * stats[...], keepdims=True) + 1e-06)
    eye = (lax.broadcasted_iota(jnp.int32, (B, B), 0) == lax.broadcasted_iota(jnp.int32, (B, B), 1))

    def factor_of(m):
        return jnp.where(eye, 1.25, 0.0) - 0.25 * m

    def advance(factor, m):
        square = split(product(factor, factor))
        fourth = split(product(square, square))
        moving[...] = product(fourth, split(m))

    m = scale * stats[...]
    start = factor_of(m)
    root[...] = start
    advance(split(start), m)

    def sweep(_, carry):
        m = moving[...]
        factor = split(factor_of(m))
        root[...] = product(split(root[...]), factor)
        advance(factor, m)
        return carry

    lax.fori_loop(0, ITERS - 2, sweep, 0)
    last = product(split(root[...]), split(factor_of(moving[...])))
    roots[...] = jnp.sqrt(jnp.sqrt(scale)) * last


def finished(tri, old):
    whole = pl.BlockSpec(memory_space=pltpu.VMEM)
    return pl.pallas_call(
        newton,
        out_shape=(jax.ShapeDtypeStruct((B, B), jnp.float32),) * 2,
        in_specs=[whole, whole],
        out_specs=(whole, whole),
        scratch_shapes=[pltpu.VMEM((B, B), jnp.float32)] * 2,
        compiler_params=pltpu.CompilerParams(vmem_limit_bytes=48 * 1024 * 1024),
        cost_estimate=pl.CostEstimate(flops=13 * 10**9, bytes_accessed=4 * 10**6, transcendentals=0),
        name="newton",
    )(tri, old)


def local(gradients, old_stats, owner_table):
    tri = routed(owner_table, gradients[0])
    stats, roots = finished(tri, old_stats[0, 0])
    return (stats[None, None], roots[None, None])


def solution(mesh):
    placed = (P("dp", "factor", None, None), P("dp", "factor", None, None), P())
    return jax.shard_map(
        local,
        mesh=mesh,
        in_specs=placed,
        out_specs=(P("dp", "factor", None, None), P("dp", "factor", None, None)),
        check_vma=False,
    )
```

time: 147 us -> 132 us (0.90); the launches traced: 146 us -> 132 us
  Pallas kernels: 141 us -> 131 us
  other arithmetic: 1.96 us -> 0 us
    pallas_call x1, Pallas kernels: 125 us -> 118 us  [routed(): pl.pallas_call(route, out_shape=jax.ShapeDtypeStruct((16,) + tile, jnp.fl...]
    pallas_call x1, Pallas kernels: 15.8 us -> 13.1 us  [finished(): pl.pallas_call(newton, out_shape=(jax.ShapeDtypeStruct((B, B), jnp.float3...]
where the time goes in v2:
time: 132 us
  Pallas kernels  131 us (99%)
    pallas_call x1, Pallas kernels, routed(): pl.pallas_call(route, out_shape=jax.ShapeDtypeStruct((16,) + tile, jnp.fl...  118 us
    pallas_call x1, Pallas kernels, finished(): pl.pallas_call(newton, out_shape=(jax.ShapeDtypeStruct((B, B), jnp.float3...  13.1 us

profile of v2, /device:TPU:1, one launch (start us, length us, event | category | flops | bytes accessed | tf_op | source)
XLA Modules:
  0.0 132.3 jit_solution(16143400192838675129)
XLA Ops:
  0.6 0.0 copy-start
  0.6 117.6 %route.1.tri = f32[16,9,8,128]{3,2,1,0:T(8,128)} custom-call(s32[16,16]{1,0:T(8,128)} %table.1, bf16[8,512,512]{2,1,0:T(8,128)(2,1)} %bitcast.5), custom_call_target="tpu_custom_call" | custom-call | flops 4000000000 | bytes 8000000 | tf_op jit(solution)/shard_map/route/pallas_call | solution.py:247
  118.2 0.0 copy-done
  118.2 0.0 copy-start.1
  118.2 1.1 copy-done.1
  119.3 13.1 %newton.1 = (f32[512,512]{1,0:T(8,128)}, f32[512,512]{1,0:T(8,128)}) custom-call(f32[16,9,8,128]{3,2,1,0:T(8,128)S(1)} %copy-done.1, f32[512,512]{1,0:T(8,128)S(1)} %bitcast.4), custom_call_target="tpu_custom_call" | custom-call | flops 12999999488 | bytes 4000000 | tf_op jit(solution)/shard_map/newton/pallas_call | solution.py:358
Async XLA Ops:
  0.6 117.6 %copy-start = (f32[1,1,512,512]{3,2,1,0:T(8,128)S(1)}, f32[1,1,512,512]{3,2,1,0:T(8,128)}, u32[]{:S(2)}) copy-start(f32[1,1,512,512]{3,2,1,0:T(8,128)} %param.4) | copy-start | bytes 3145732
  118.2 1.1 copy-start.1

commit v3 on v2

--- a/solution.py
+++ b/solution.py
@@ -30,8 +30,8 @@
     return jnp.concatenate([block[:, T // 2:], block[:, :T // 2]], axis=1)
 
 
-def route(table, grads, out, xg, part, r1, r2, xt, fs, fr, ds, dr, items, columns,
-          own_sem, xs, xr, zs, zr, ts, tr, as_, ar, bs, br, turn):
+def route(table, grads, out, xg, part, r1, r2, r3, xt, fs, fr, ds, dr, items, columns,
+          own_sem, xs, xr, zs, zr, ws, wr, ts, tr, as_, ar, bs, br, turn):
     d = lax.axis_index("dp")
     f = lax.axis_index("factor")
     x, zl = d // 4, d % 4
@@ -65,13 +65,6 @@
     for copy in own:
         copy.start()
 
-    owners = [table[f, j] for j in range(16)]
-    for g in range(16):
-        pick = jnp.int32(0)
-        for j in range(16):
-            pick = jnp.where(lax.shift_right_logical(owners[j], 4) == g, j, pick)
-        items[g] = pick
-
     def find_column(e, carry):
         def scan(c, found):
             for j in range(16):
@@ -89,12 +82,19 @@
 
     def z_copy(c, side, step):
         if step == 0:
-            src, dst = part.at[c, side, pl.ds((1 - b0) * 8, 8)], r1.at[c, side]
+            src, dst = part.at[c, side, pl.ds((1 - b0) * 8, 8)], r1.at[side]
         else:
-            src, dst = part.at[c, side, pl.ds(b0 * 8 + (1 - b1) * 4, 4)], r2.at[c, side]
-        return pltpu.make_async_remote_copy(
-            src_ref=src, dst_ref=dst, send_sem=zs.at[c, side, step], recv_sem=zr.at[c, side, step],
+            src, dst = part.at[c, side, pl.ds(b0 * 8 + (1 - b1) * 4, 4)], r2.at[side]
+        return pltpu.make_async_remote_copy(
+            src_ref=src, dst_ref=dst, send_sem=zs.at[side, step], recv_sem=zr.at[side, step],
             device_id=z_peer(step), device_id_type=MESH)
+
+    def w_copy(side, k):
+        to = (q + k) % 4
+        return pltpu.make_async_remote_copy(
+            src_ref=part.at[1, side, pl.ds((to % 2) * 8 + (to // 2) * 4, 4)], dst_ref=r3.at[side, k],
+            send_sem=ws.at[side, k], recv_sem=wr.at[side, k],
+            device_id={"dp": dp_at(x, to, zh), "factor": f}, device_id_type=MESH)
 
     def t_copy(c, side, k):
         return pltpu.make_async_remote_copy(
@@ -152,12 +152,6 @@
                         block = jnp.where(low_left(), corner_parts[i], block)
                     part[c, side, :, n] = block.reshape(16, 8, T)
 
-    def fold(c, side, step):
-        if step == 0:
-            part[c, side, pl.ds(b0 * 8, 8)] += r1[c, side]
-        else:
-            part[c, side, pl.ds(home, 4)] += r2[c, side]
-
     def spread(c, side):
         for k in order:
             t_copy(c, side, k).start()
@@ -182,34 +176,41 @@
         pl.semaphore_wait(turn, 1)
         send_x()
 
+    owners = [table[f, j] for j in range(16)]
+    for g in range(16):
+        pick = jnp.int32(0)
+        for j in range(16):
+            pick = jnp.where(lax.shift_right_logical(owners[j], 4) == g, j, pick)
+        items[g] = pick
     lax.fori_loop(0, 16, find_column, 0)
 
     def arrive(c):
         own[c].wait()
         for k in order:
             x_copy(c, k).wait_recv()
-        for side in range(2):
-            gram(c, side)
-            z_copy(c, side, 0).start()
-
-    def halve(c):
-        for side in range(2):
-            z_copy(c, side, 0).wait_recv()
-            fold(c, side, 0)
-            z_copy(c, side, 1).start()
-
-    def settle(c):
-        for side in range(2):
-            z_copy(c, side, 1).wait_recv()
-            fold(c, side, 1)
-            spread(c, side)
 
     arrive(0)
-    halve(0)
+    for side in range(2):
+        gram(0, side)
+        z_copy(0, side, 0).start()
+    for side in range(2):
+        z_copy(0, side, 0).wait_recv()
+        part[0, side, pl.ds(b0 * 8, 8)] += r1[side]
+        z_copy(0, side, 1).start()
     arrive(1)
-    settle(0)
-    halve(1)
-    settle(1)
+    for side in range(2):
+        gram(1, side)
+        for k in order:
+            w_copy(side, k).start()
+    for side in range(2):
+        z_copy(0, side, 1).wait_recv()
+        part[0, side, pl.ds(home, 4)] += r2[side]
+        spread(0, side)
+    for side in range(2):
+        for k in order:
+            w_copy(side, k).wait_recv()
+        part[1, side, pl.ds(home, 4)] += (r3[side, 1] + r3[side, 2]) + r3[side, 3]
+        spread(1, side)
     for c in range(2):
         for side in range(2):
             for k in order:
@@ -233,10 +234,13 @@
 
     for c in range(2):
         for side in range(2):
-            for step in range(2):
-                z_copy(c, side, step).wait_send()
             for k in order:
                 t_copy(c, side, k).wait_send()
+    for side in range(2):
+        for step in range(2):
+            z_copy(0, side, step).wait_send()
+        for k in order:
+            w_copy(side, k).wait_send()
     for k in range(1, 16):
         a_copy((f + k) % 16).wait_send()
         b_copy((d + k) % 16).wait_send()
@@ -255,8 +259,9 @@
         scratch_shapes=[
             pltpu.VMEM((2, 4, B, B), jnp.bfloat16),
             pltpu.VMEM((2, 2, 16) + tile, jnp.float32),
-            pltpu.VMEM((2, 2, 8) + tile, jnp.float32),
-            pltpu.VMEM((2, 2, 4) + tile, jnp.float32),
+            pltpu.VMEM((2, 8) + tile, jnp.float32),
+            pltpu.VMEM((2, 4) + tile, jnp.float32),
+            pltpu.VMEM((2, 4, 4) + tile, jnp.float32),
             pltpu.VMEM((16,) + tile, jnp.float32),
             pltpu.VMEM((16,) + tile, jnp.float32),
             pltpu.VMEM((16,) + tile, jnp.float32),
@@ -267,8 +272,10 @@
             pltpu.SemaphoreType.DMA((2,)),
             pltpu.SemaphoreType.DMA((2, 4)),
             pltpu.SemaphoreType.DMA((2, 4)),
-            pltpu.SemaphoreType.DMA((2, 2, 2)),
-            pltpu.SemaphoreType.DMA((2, 2, 2)),
+            pltpu.SemaphoreType.DMA((2, 2)),
+            pltpu.SemaphoreType.DMA((2, 2)),
+            pltpu.SemaphoreType.DMA((2, 4)),
+            pltpu.SemaphoreType.DMA((2, 4)),
             pltpu.SemaphoreType.DMA((2, 2, 4)),
             pltpu.SemaphoreType.DMA((2, 2, 4)),
             pltpu.SemaphoreType.DMA((16,)),
@@ -278,7 +285,7 @@
             pltpu.SemaphoreType.REGULAR,
         ],
         compiler_params=pltpu.CompilerParams(
-            collective_id=0, has_side_effects=True, vmem_limit_bytes=60 * 1024 * 1024
+            collective_id=0, has_side_effects=True, vmem_limit_bytes=52 * 1024 * 1024
         ),
         cost_estimate=pl.CostEstimate(flops=4 * 10**9, bytes_accessed=8 * 10**6, transcendentals=0),
         name="route",
@@ -290,21 +297,25 @@
     return high, (a - high.astype(jnp.float32)).astype(jnp.bfloat16)
 
 
-def dot(left, right):
-    return jnp.dot(left, right, preferred_element_type=jnp.float32)
+def halves(matrix):
+    return {place: split(quarter) for place, quarter in matrix.items()}
 
 
 def product(a, b):
-    def quad(r, c):
-        rows, cols = slice(r * H, (r + 1) * H), slice(c * H, (c + 1) * H)
-        return dot(a[0][rows], b[0][:, cols]) + (dot(a[0][rows], b[1][:, cols]) + dot(a[1][rows], b[0][:, cols]))
-
-    upper = quad(0, 1)
-    top = jnp.concatenate([quad(0, 0), upper], axis=1)
-    return jnp.concatenate([top, jnp.concatenate([upper.T, quad(1, 1)], axis=1)], axis=0)
-
-
-def newton(tri, old, stats, roots, moving, root):
+    out = {}
+    for r, c in ((0, 0), (0, 1), (1, 1)):
+        left, right = [], []
+        for k in range(2):
+            left += [a[r, k][0], a[r, k][0], a[r, k][1]]
+            right += [b[k, c][0], b[k, c][1], b[k, c][0]]
+        out[r, c] = jnp.dot(
+            jnp.concatenate(left, axis=1), jnp.concatenate(right, axis=0), preferred_element_type=jnp.float32
+        )
+    out[1, 0] = out[0, 1].T
+    return out
+
+
+def newton(tri, old, stats, roots):
     def blend(i, j, block):
         rows, cols = slice(i * T, (i + 1) * T), slice(j * T, (j + 1) * T)
         stats[rows, cols] = BETA * old[rows, cols] + (1.0 - BETA) * block
@@ -326,31 +337,28 @@
     blend(3, 3, jnp.where(mask, corner.T, corner))
 
     scale = 2.5 / jnp.sqrt(jnp.sum(stats[...] * stats[...], keepdims=True) + 1e-06)
-    eye = (lax.broadcasted_iota(jnp.int32, (B, B), 0) == lax.broadcasted_iota(jnp.int32, (B, B), 1))
-
-    def factor_of(m):
-        return jnp.where(eye, 1.25, 0.0) - 0.25 * m
-
-    def advance(factor, m):
-        square = split(product(factor, factor))
-        fourth = split(product(square, square))
-        moving[...] = product(fourth, split(m))
-
-    m = scale * stats[...]
-    start = factor_of(m)
-    root[...] = start
-    advance(split(start), m)
-
-    def sweep(_, carry):
-        m = moving[...]
-        factor = split(factor_of(m))
-        root[...] = product(split(root[...]), factor)
-        advance(factor, m)
-        return carry
-
-    lax.fori_loop(0, ITERS - 2, sweep, 0)
-    last = product(split(root[...]), split(factor_of(moving[...])))
-    roots[...] = jnp.sqrt(jnp.sqrt(scale)) * last
+    eye = lax.broadcasted_iota(jnp.int32, (H, H), 0) == lax.broadcasted_iota(jnp.int32, (H, H), 1)
+
+    def factor_of(matrix):
+        return {
+            (r, c): (jnp.where(eye, 1.25, 0.0) if r == c else 0.0) - 0.25 * quarter
+            for (r, c), quarter in matrix.items()
+        }
+
+    moving = {
+        (r, c): scale * stats[r * H:(r + 1) * H, c * H:(c + 1) * H] for r in range(2) for c in range(2)
+    }
+    root = factor_of(moving)
+    factor = halves(root)
+    for sweep in range(1, ITERS):
+        square = halves(product(factor, factor))
+        fourth = halves(product(square, square))
+        moving = product(fourth, halves(moving))
+        factor = halves(factor_of(moving))
+        root = product(halves(root), factor)
+    post = jnp.sqrt(jnp.sqrt(scale))
+    for (r, c), quarter in root.items():
+        roots[r * H:(r + 1) * H, c * H:(c + 1) * H] = post * quarter
 
 
 def finished(tri, old):
@@ -360,7 +368,6 @@
         out_shape=(jax.ShapeDtypeStruct((B, B), jnp.float32),) * 2,
         in_specs=[whole, whole],
         out_specs=(whole, whole),
-        scratch_shapes=[pltpu.VMEM((B, B), jnp.float32)] * 2,
         compiler_params=pltpu.CompilerParams(vmem_limit_bytes=48 * 1024 * 1024),
         cost_estimate=pl.CostEstimate(flops=13 * 10**9, bytes_accessed=4 * 10**6, transcendentals=0),
         name="newton",

time: 132 us -> 130 us (0.985)
  Pallas kernels: 131 us -> 128 us
where the time goes in v3:
time: 130 us
  Pallas kernels  128 us (98%)
    pallas_call x1, Pallas kernels, routed(): pl.pallas_call(route, out_shape=jax.ShapeDtypeStruct((16,) + tile, jnp.fl...  116 us
    pallas_call x1, Pallas kernels, finished(): pl.pallas_call(newton, out_shape=(jax.ShapeDtypeStruct((B, B), jnp.float3...  11.9 us

profile of v3, /device:TPU:1, one launch (start us, length us, event | category | flops | bytes accessed | tf_op | source)
XLA Modules:
  0.0 129.5 jit_solution(13424533583651946205)
XLA Ops:
  0.6 0.0 copy-start.1
  0.6 0.7 copy-done.1
  1.3 0.0 copy-start
  1.3 116.3 %route.1.tri = f32[16,9,8,128]{3,2,1,0:T(8,128)S(1)} custom-call(s32[16,16]{1,0:T(8,128)S(1)} %copy-done.1, bf16[8,512,512]{2,1,0:T(8,128)(2,1)} %bitcast.5), custom_call_target="tpu_custom_call" | custom-call | flops 4000000000 | bytes 8000000 | tf_op jit(solution)/shard_map/route/pallas_call | solution.py:251
  117.6 0.0 copy-done
  117.6 11.9 %newton.1 = (f32[512,512]{1,0:T(8,128)}, f32[512,512]{1,0:T(8,128)}) custom-call(f32[16,9,8,128]{3,2,1,0:T(8,128)S(1)} %route.1.tri, f32[512,512]{1,0:T(8,128)S(1)} %bitcast.4), custom_call_target="tpu_custom_call" | custom-call | flops 12999999488 | bytes 4000000 | tf_op jit(solution)/shard_map/newton/pallas_call | solution.py:366
Async XLA Ops:
  0.6 0.7 copy-start.1
  1.3 116.3 %copy-start = (f32[1,1,512,512]{3,2,1,0:T(8,128)S(1)}, f32[1,1,512,512]{3,2,1,0:T(8,128)}, u32[]{:S(2)}) copy-start(f32[1,1,512,512]{3,2,1,0:T(8,128)} %param.4) | copy-start | bytes 3145732

commit v4 on v3

--- a/solution.py
+++ b/solution.py
@@ -30,7 +30,7 @@
     return jnp.concatenate([block[:, T // 2:], block[:, :T // 2]], axis=1)
 
 
-def route(table, grads, out, xg, part, r1, r2, r3, xt, fs, fr, ds, dr, items, columns,
+def route(table, grads, out, xg, part, last, r1, r2, r3, xt, fs, fr, ds, dr, items, columns,
           own_sem, xs, xr, zs, zr, ws, wr, ts, tr, as_, ar, bs, br, turn):
     d = lax.axis_index("dp")
     f = lax.axis_index("factor")
@@ -80,26 +80,34 @@
             src_ref=grads.at[2 * ((x + k) % 4) + c], dst_ref=xg.at[c, k],
             send_sem=xs.at[c, k], recv_sem=xr.at[c, k], device_id=x_peer(k), device_id_type=MESH)
 
-    def z_copy(c, side, step):
+    def z_copy(side, step):
         if step == 0:
-            src, dst = part.at[c, side, pl.ds((1 - b0) * 8, 8)], r1.at[side]
+            src, dst = part.at[side, pl.ds((1 - b0) * 8, 8)], r1.at[side]
         else:
-            src, dst = part.at[c, side, pl.ds(b0 * 8 + (1 - b1) * 4, 4)], r2.at[side]
+            src, dst = part.at[side, pl.ds(b0 * 8 + (1 - b1) * 4, 4)], r2.at[side]
         return pltpu.make_async_remote_copy(
             src_ref=src, dst_ref=dst, send_sem=zs.at[side, step], recv_sem=zr.at[side, step],
             device_id=z_peer(step), device_id_type=MESH)
 
-    def w_copy(side, k):
-        to = (q + k) % 4
-        return pltpu.make_async_remote_copy(
-            src_ref=part.at[1, side, pl.ds((to % 2) * 8 + (to // 2) * 4, 4)], dst_ref=r3.at[side, k],
-            send_sem=ws.at[side, k], recv_sem=wr.at[side, k],
-            device_id={"dp": dp_at(x, to, zh), "factor": f}, device_id_type=MESH)
-
-    def t_copy(c, side, k):
-        return pltpu.make_async_remote_copy(
-            src_ref=part.at[c, side, home + (x + k) % 4], dst_ref=xt.at[4 * x + 2 * c + side],
-            send_sem=ts.at[c, side, k], recv_sem=tr.at[c, side, k], device_id=x_peer(k), device_id_type=MESH)
+    def t_copy(side, k):
+        return pltpu.make_async_remote_copy(
+            src_ref=part.at[side, home + (x + k) % 4], dst_ref=xt.at[4 * x + side],
+            send_sem=ts.at[side, k], recv_sem=tr.at[side, k], device_id=x_peer(k), device_id_type=MESH)
+
+    def piece_of(e):
+        e_x, e_zl = e // 4, e % 4
+        e_q = e_zl + zh * (3 - 2 * e_zl)
+        return (e_q % 2) * 8 + (e_q // 2) * 4 + e_x
+
+    def w_copy(e):
+        return pltpu.make_async_remote_copy(
+            src_ref=last.at[piece_of(e)], dst_ref=r3.at[d], send_sem=ws.at[e], recv_sem=wr.at[d],
+            device_id=d_peer(e), device_id_type=MESH)
+
+    def w_landed(e):
+        return pltpu.make_async_remote_copy(
+            src_ref=last.at[piece_of(e)], dst_ref=r3.at[e], send_sem=ws.at[e], recv_sem=wr.at[e],
+            device_id=d_peer(e), device_id_type=MESH)
 
     def a_copy(g):
         return pltpu.make_async_remote_copy(
@@ -117,9 +125,7 @@
             device_id=d_peer(e), device_id_type=MESH)
 
     def b_landed(e):
-        e_x, e_zl = e // 4, e % 4
-        e_q = e_zl + zh * (3 - 2 * e_zl)
-        e_piece = (e_q % 2) * 8 + (e_q // 2) * 4 + e_x
+        e_piece = piece_of(e)
         return pltpu.make_async_remote_copy(
             src_ref=ds.at[e], dst_ref=dr.at[e_piece], send_sem=bs.at[e], recv_sem=br.at[e_piece],
             device_id=d_peer(e), device_id_type=MESH)
@@ -150,71 +156,76 @@
                     block = total[i0:i0 + T, j0:j0 + T]
                     if i == j:
                         block = jnp.where(low_left(), corner_parts[i], block)
-                    part[c, side, :, n] = block.reshape(16, 8, T)
-
-    def spread(c, side):
-        for k in order:
-            t_copy(c, side, k).start()
-        xt[4 * x + 2 * c + side] = part[c, side, piece]
+                    if c == 0:
+                        part[side, :, n] = block.reshape(16, 8, T)
+                    else:
+                        last[:, side, n] = block.reshape(16, 8, T)
 
     order = (2, 1, 3)
-
-    def send_x():
-        for c in range(2):
-            for k in order:
-                x_copy(c, k).start()
-            for k in order:
-                x_copy(c, k).wait_send()
-
-    @pl.when(core == 0)
-    def _():
-        send_x()
-        pl.semaphore_signal(turn, inc=1, device_id={"dp": d, "factor": f + 1}, device_id_type=MESH)
+    partner = {"dp": d, "factor": f + 1 - 2 * core}
+
+    def send_x(c):
+        for k in order:
+            x_copy(c, k).start()
+
+    def sent_x(c):
+        for k in order:
+            x_copy(c, k).wait_send()
+
+    def arrive(c):
+        own[c].wait()
+        for k in order:
+            x_copy(c, k).wait_recv()
 
     @pl.when(core == 1)
     def _():
         pl.semaphore_wait(turn, 1)
-        send_x()
-
-    owners = [table[f, j] for j in range(16)]
+
+    send_x(0)
     for g in range(16):
         pick = jnp.int32(0)
         for j in range(16):
-            pick = jnp.where(lax.shift_right_logical(owners[j], 4) == g, j, pick)
+            pick = jnp.where(lax.shift_right_logical(table[f, j], 4) == g, j, pick)
         items[g] = pick
     lax.fori_loop(0, 16, find_column, 0)
-
-    def arrive(c):
-        own[c].wait()
-        for k in order:
-            x_copy(c, k).wait_recv()
+    sent_x(0)
+    pl.semaphore_signal(turn, inc=1, device_id=partner, device_id_type=MESH)
 
     arrive(0)
     for side in range(2):
         gram(0, side)
-        z_copy(0, side, 0).start()
-    for side in range(2):
-        z_copy(0, side, 0).wait_recv()
-        part[0, side, pl.ds(b0 * 8, 8)] += r1[side]
-        z_copy(0, side, 1).start()
+        z_copy(side, 0).start()
+    for side in range(2):
+        z_copy(side, 0).wait_recv()
+        part[side, pl.ds(b0 * 8, 8)] += r1[side]
+        z_copy(side, 1).start()
+    pl.semaphore_wait(turn, 1)
+    send_x(1)
+    for side in range(2):
+        z_copy(side, 1).wait_recv()
+        part[side, pl.ds(home, 4)] += r2[side]
+        for k in order:
+            t_copy(side, k).start()
+        xt[4 * x + side] = part[side, piece]
+    sent_x(1)
+
+    @pl.when(core == 0)
+    def _():
+        pl.semaphore_signal(turn, inc=1, device_id=partner, device_id_type=MESH)
+
     arrive(1)
     for side in range(2):
         gram(1, side)
-        for k in order:
-            w_copy(side, k).start()
-    for side in range(2):
-        z_copy(0, side, 1).wait_recv()
-        part[0, side, pl.ds(home, 4)] += r2[side]
-        spread(0, side)
-    for side in range(2):
-        for k in order:
-            w_copy(side, k).wait_recv()
-        part[1, side, pl.ds(home, 4)] += (r3[side, 1] + r3[side, 2]) + r3[side, 3]
-        spread(1, side)
-    for c in range(2):
-        for side in range(2):
-            for k in order:
-                t_copy(c, side, k).wait_recv()
+    for k in range(1, 16):
+        w_copy((d + k) % 16).start()
+    r3[d] = last[piece]
+    for side in range(2):
+        for k in order:
+            t_copy(side, k).wait_recv()
+    for k in range(1, 16):
+        w_landed((d + k) % 16).wait_recv()
+    for i in range(4):
+        xt[4 * i + 2:4 * i + 4] = (r3[4 * i] + r3[4 * i + 1]) + (r3[4 * i + 2] + r3[4 * i + 3])
 
     for k in range(1, 16):
         g = (f + k) % 16
@@ -232,15 +243,13 @@
         b_landed((d + k) % 16).wait_recv()
     out[...] = dr[...]
 
-    for c in range(2):
-        for side in range(2):
-            for k in order:
-                t_copy(c, side, k).wait_send()
     for side in range(2):
         for step in range(2):
-            z_copy(0, side, step).wait_send()
-        for k in order:
-            w_copy(side, k).wait_send()
+            z_copy(side, step).wait_send()
+        for k in order:
+            t_copy(side, k).wait_send()
+    for k in range(1, 16):
+        w_copy((d + k) % 16).wait_send()
     for k in range(1, 16):
         a_copy((f + k) % 16).wait_send()
         b_copy((d + k) % 16).wait_send()
@@ -258,10 +267,11 @@
         out_specs=pl.BlockSpec(memory_space=pltpu.VMEM),
         scratch_shapes=[
             pltpu.VMEM((2, 4, B, B), jnp.bfloat16),
-            pltpu.VMEM((2, 2, 16) + tile, jnp.float32),
+            pltpu.VMEM((2, 16) + tile, jnp.float32),
+            pltpu.VMEM((16, 2) + tile, jnp.float32),
             pltpu.VMEM((2, 8) + tile, jnp.float32),
             pltpu.VMEM((2, 4) + tile, jnp.float32),
-            pltpu.VMEM((2, 4, 4) + tile, jnp.float32),
+            pltpu.VMEM((16, 2) + tile, jnp.float32),
             pltpu.VMEM((16,) + tile, jnp.float32),
             pltpu.VMEM((16,) + tile, jnp.float32),
             pltpu.VMEM((16,) + tile, jnp.float32),
@@ -274,10 +284,10 @@
             pltpu.SemaphoreType.DMA((2, 4)),
             pltpu.SemaphoreType.DMA((2, 2)),
             pltpu.SemaphoreType.DMA((2, 2)),
+            pltpu.SemaphoreType.DMA((16,)),
+            pltpu.SemaphoreType.DMA((16,)),
             pltpu.SemaphoreType.DMA((2, 4)),
             pltpu.SemaphoreType.DMA((2, 4)),
-            pltpu.SemaphoreType.DMA((2, 2, 4)),
-            pltpu.SemaphoreType.DMA((2, 2, 4)),
             pltpu.SemaphoreType.DMA((16,)),
             pltpu.SemaphoreType.DMA((16,)),
             pltpu.SemaphoreType.DMA((16,)),

time: 130 us -> 121 us (0.931)
  Pallas kernels: 128 us -> 120 us
    pallas_call x1, Pallas kernels: 116 us -> 108 us  [routed(): pl.pallas_call(route, out_shape=jax.ShapeDtypeStruct((16,) + tile, jnp.fl...]
where the time goes in v4:
time: 121 us
  Pallas kernels  120 us (99%)
    pallas_call x1, Pallas kernels, routed(): pl.pallas_call(route, out_shape=jax.ShapeDtypeStruct((16,) + tile, jnp.fl...  108 us
    pallas_call x1, Pallas kernels, finished(): pl.pallas_call(newton, out_shape=(jax.ShapeDtypeStruct((B, B), jnp.float3...  11.7 us

profile of v4, /device:TPU:1, one launch (start us, length us, event | category | flops | bytes accessed | tf_op | source)
XLA Modules:
  0.0 121.2 jit_solution(17936970831623563642)
XLA Ops:
  0.6 0.0 copy-start.1
  0.6 0.7 copy-done.1
  1.3 0.0 copy-start
  1.3 108.2 %route.1.tri = f32[16,9,8,128]{3,2,1,0:T(8,128)S(1)} custom-call(s32[16,16]{1,0:T(8,128)S(1)} %copy-done.1, bf16[8,512,512]{2,1,0:T(8,128)(2,1)} %bitcast.5), custom_call_target="tpu_custom_call" | custom-call | flops 4000000000 | bytes 8000000 | tf_op jit(solution)/shard_map/route/pallas_call | solution.py:260
  109.5 0.0 copy-done
  109.5 11.7 %newton.1 = (f32[512,512]{1,0:T(8,128)}, f32[512,512]{1,0:T(8,128)}) custom-call(f32[16,9,8,128]{3,2,1,0:T(8,128)S(1)} %route.1.tri, f32[512,512]{1,0:T(8,128)S(1)} %bitcast.4), custom_call_target="tpu_custom_call" | custom-call | flops 12999999488 | bytes 4000000 | tf_op jit(solution)/shard_map/newton/pallas_call | solution.py:376
Async XLA Ops:
  0.6 0.7 copy-start.1
  1.3 108.2 %copy-start = (f32[1,1,512,512]{3,2,1,0:T(8,128)S(1)}, f32[1,1,512,512]{3,2,1,0:T(8,128)}, u32[]{:S(2)}) copy-start(f32[1,1,512,512]{3,2,1,0:T(8,128)} %param.4) | copy-start | bytes 3145732

commit v5 on v4

v5 whole, which is shorter than its diff:
```python
import jax
import jax.numpy as jnp
from jax import lax
from jax.experimental import pallas as pl
from jax.experimental.pallas import tpu as pltpu
from jax.sharding import PartitionSpec as P

ITERS = 5
BETA = 0.9
B = 512
T = 128
MESH = pl.DeviceIdType.MESH
PARTS = (((0, 2), (0, 3), (1, 2), (1, 3)), ((0, 1), (2, 3), (0, 0), (1, 1), (2, 2)))
QUADS = (((0, 1),), ((1, 1), (0, 0)))
H = 256


def low_left():
    rows = lax.broadcasted_iota(jnp.int32, (T, T), 0)
    cols = lax.broadcasted_iota(jnp.int32, (T, T), 1)
    return jnp.logical_and(rows >= T // 2, cols < T // 2)


def swapped(block):
    return jnp.concatenate([block[T // 2:], block[:T // 2]], axis=0)


def turned(block):
    return jnp.concatenate([block[:, T // 2:], block[:, :T // 2]], axis=1)


def route(table, grads, out0, out1, xg, part0, part1, last0, last1, r10, r11, r20, r21, r30, r31, xt0, xt1, fs0, fs1, fr0, fr1,
          ds0, ds1, dr0, dr1, items, columns, own_sem, xs, xr, zs, zr, ws, wr, ts, tr, as_, ar, bs, br, turn):
    r1, r2 = (r10, r11), (r20, r21)
    part, last, r3, xt = (part0, part1), (last0, last1), (r30, r31), (xt0, xt1)
    fs, fr, ds, dr, out = (fs0, fs1), (fr0, fr1), (ds0, ds1), (dr0, dr1), (out0, out1)
    d = lax.axis_index("dp")
    f = lax.axis_index("factor")
    x, zl = d // 4, d % 4
    zh, core = f // 8, f % 2
    q = zl + zh * (3 - 2 * zl)
    b0, b1 = q % 2, q // 2
    home = b0 * 8 + b1 * 4
    piece = home + x

    def dp_at(x_, q_, zh_):
        return x_ * 4 + q_ + zh_ * (3 - 2 * q_)

    def x_peer(k):
        return {"dp": dp_at((x + k) % 4, q, zh), "factor": f}

    def z_peer(step):
        flip = q + 1 - 2 * b0 if step == 0 else q + 2 - 4 * b1
        return {"dp": dp_at(x, flip, zh), "factor": f}

    def f_peer(g):
        return {"dp": dp_at(x, q, g // 8), "factor": g}

    def d_peer(e):
        return {"dp": e, "factor": f}

    barrier = pltpu.get_barrier_semaphore()
    for k in range(1, 16):
        pl.semaphore_signal(barrier, inc=1, device_id=d_peer((d + k) % 16), device_id_type=MESH)
        pl.semaphore_signal(barrier, inc=1, device_id=f_peer((f + k) % 16), device_id_type=MESH)
    own = [pltpu.make_async_copy(grads.at[2 * x + c], xg.at[c, 0], own_sem.at[c]) for c in range(2)]
    for copy in own:
        copy.start()

    def find_column(e, carry):
        def scan(c, found):
            for j in range(16):
                found = jnp.where(table[c, j] == f * 16 + e, c, found)
            return found
        columns[e] = lax.fori_loop(0, 16, scan, jnp.int32(0))
        return carry

    pl.semaphore_wait(barrier, 30)

    def x_copy(c, k):
        return pltpu.make_async_remote_copy(
            src_ref=grads.at[2 * ((x + k) % 4) + c], dst_ref=xg.at[c, k],
            send_sem=xs.at[c, k], recv_sem=xr.at[c, k], device_id=x_peer(k), device_id_type=MESH)

    def z_copy(h, step):
        if step == 0:
            src, dst = part[h].at[pl.ds((1 - b0) * 8, 8)], r1[h]
        else:
            src, dst = part[h].at[pl.ds(b0 * 8 + (1 - b1) * 4, 4)], r2[h]
        return pltpu.make_async_remote_copy(
            src_ref=src, dst_ref=dst, send_sem=zs.at[h, step], recv_sem=zr.at[h, step],
            device_id=z_peer(step), device_id_type=MESH)

    def t_copy(h, k):
        return pltpu.make_async_remote_copy(
            src_ref=part[h].at[home + (x + k) % 4], dst_ref=xt[h].at[pl.ds(4 * x, 2)],
            send_sem=ts.at[h, k], recv_sem=tr.at[h, k], device_id=x_peer(k), device_id_type=MESH)

    def piece_of(e):
        e_x, e_zl = e // 4, e % 4
        e_q = e_zl + zh * (3 - 2 * e_zl)
        return (e_q % 2) * 8 + (e_q // 2) * 4 + e_x

    def w_copy(h, e):
        return pltpu.make_async_remote_copy(
            src_ref=last[h].at[piece_of(e)], dst_ref=r3[h].at[d], send_sem=ws.at[h, e], recv_sem=wr.at[h, d],
            device_id=d_peer(e), device_id_type=MESH)

    def w_landed(h, e):
        return pltpu.make_async_remote_copy(
            src_ref=last[h].at[piece_of(e)], dst_ref=r3[h].at[e], send_sem=ws.at[h, e], recv_sem=wr.at[h, e],
            device_id=d_peer(e), device_id_type=MESH)

    def a_copy(h, g):
        return pltpu.make_async_remote_copy(
            src_ref=fs[h].at[g], dst_ref=fr[h].at[f], send_sem=as_.at[h, g], recv_sem=ar.at[h, f],
            device_id=f_peer(g), device_id_type=MESH)

    def a_landed(h, g):
        return pltpu.make_async_remote_copy(
            src_ref=fs[h].at[g], dst_ref=fr[h].at[g], send_sem=as_.at[h, g], recv_sem=ar.at[h, g],
            device_id=f_peer(g), device_id_type=MESH)

    def b_copy(h, e):
        return pltpu.make_async_remote_copy(
            src_ref=ds[h].at[e], dst_ref=dr[h].at[piece], send_sem=bs.at[h, e], recv_sem=br.at[h, piece],
            device_id=d_peer(e), device_id_type=MESH)

    def b_landed(h, e):
        e_piece = piece_of(e)
        return pltpu.make_async_remote_copy(
            src_ref=ds[h].at[e], dst_ref=dr[h].at[e_piece], send_sem=bs.at[h, e], recv_sem=br.at[h, e_piece],
            device_id=d_peer(e), device_id_type=MESH)

    def gram(c, h, side):
        corner = None
        for row, col in QUADS[h]:
            total = None
            for k in range(4):
                if side == 0:
                    left = xg[c, k, row * H:(row + 1) * H, :]
                    right = xg[c, k, col * H:(col + 1) * H, :]
                    dims = (((1,), (1,)), ((), ()))
                else:
                    left = xg[c, k, :, row * H:(row + 1) * H]
                    right = xg[c, k, :, col * H:(col + 1) * H]
                    dims = (((0,), (0,)), ((), ()))
                term = lax.dot_general(left, right, dims, preferred_element_type=jnp.float32)
                total = term if total is None else total + term
            if (row, col) == (1, 1):
                corner = total[T:, T:]
                shifted = swapped(corner)
                corner_parts = (shifted, turned(shifted), turned(corner))
            for n, (i, j) in enumerate(PARTS[h]):
                if i // 2 == row and j // 2 == col:
                    i0, j0 = (i % 2) * T, (j % 2) * T
                    block = total[i0:i0 + T, j0:j0 + T]
                    if i == j:
                        block = jnp.where(low_left(), corner_parts[i], block)
                    kept = part if c == 0 else last
                    kept[h][:, side, n] = block.reshape(16, 8, T)

    order = (2, 1, 3)
    partner = {"dp": d, "factor": f + 1 - 2 * core}

    def send_x(c):
        for k in order:
            x_copy(c, k).start()

    def arrive(c):
        own[c].wait()
        for k in order:
            x_copy(c, k).wait_recv()

    @pl.when(core == 1)
    def _():
        pl.semaphore_wait(turn, 1)

    send_x(0)
    for g in range(16):
        pick = jnp.int32(0)
        for j in range(16):
            pick = jnp.where(lax.shift_right_logical(table[f, j], 4) == g, j, pick)
        items[g] = pick
    lax.fori_loop(0, 16, find_column, 0)
    x_copy(0, 1).wait_send()
    pl.semaphore_signal(turn, inc=1, device_id=partner, device_id_type=MESH)

    arrive(0)
    for h in range(2):
        for side in range(2):
            gram(0, h, side)
        z_copy(h, 0).start()
    for h in range(2):
        z_copy(h, 0).wait_recv()
        part[h][pl.ds(b0 * 8, 8)] += r1[h][...]
        z_copy(h, 1).start()
    pl.semaphore_wait(turn, 1)
    send_x(1)
    for h in range(2):
        z_copy(h, 1).wait_recv()
        part[h][pl.ds(home, 4)] += r2[h][...]
        for k in order:
            t_copy(h, k).start()
        xt[h][pl.ds(4 * x, 2)] = part[h][piece]
    x_copy(1, 1).wait_send()

    @pl.when(core == 0)
    def _():
        pl.semaphore_signal(turn, inc=1, device_id=partner, device_id_type=MESH)

    arrive(1)
    for h in range(2):
        for side in range(2):
            gram(1, h, side)
        for k in range(1, 16):
            w_copy(h, (d + k) % 16).start()
        r3[h][d] = last[h][piece]
    for h in range(2):
        for k in order:
            t_copy(h, k).wait_recv()
    for h in range(2):
        for k in range(1, 16):
            w_landed(h, (d + k) % 16).wait_recv()
        for i in range(4):
            here = r3[h][4 * i:4 * i + 4]
            xt[h][4 * i + 2:4 * i + 4] = (here[0] + here[1]) + (here[2] + here[3])
        for k in range(1, 16):
            g = (f + k) % 16
            fs[h][g] = xt[h][items[g]]
            a_copy(h, g).start()
        fr[h][f] = xt[h][items[f]]
    for h in range(2):
        for k in range(1, 16):
            a_landed(h, (f + k) % 16).wait_recv()
        for k in range(1, 16):
            e = (d + k) % 16
            ds[h][e] = fr[h][columns[e]]
            b_copy(h, e).start()
        dr[h][piece] = fr[h][columns[d]]
    for h in range(2):
        for k in range(1, 16):
            b_landed(h, (d + k) % 16).wait_recv()
        out[h][...] = dr[h][...]

    for c in range(2):
        for k in (2, 3):
            x_copy(c, k).wait_send()
    for h in range(2):
        for step in range(2):
            z_copy(h, step).wait_send()
        for k in order:
            t_copy(h, k).wait_send()
        for k in range(1, 16):
            w_copy(h, (d + k) % 16).wait_send()
            a_copy(h, (f + k) % 16).wait_send()
            b_copy(h, (d + k) % 16).wait_send()


def routed(table, grads):
    tiles = [(len(blocks), 8, T) for blocks in PARTS]

    def buffers(*lead):
        return [pltpu.VMEM(lead + tile, jnp.float32) for tile in tiles]

    def semaphores(*shape):
        return [pltpu.SemaphoreType.DMA(shape)] * 2

    return pl.pallas_call(
        route,
        out_shape=tuple(jax.ShapeDtypeStruct((16,) + tile, jnp.float32) for tile in tiles),
        in_specs=[
            pl.BlockSpec(memory_space=pltpu.SMEM),
            pl.BlockSpec(memory_space=pltpu.HBM),
        ],
        out_specs=(pl.BlockSpec(memory_space=pltpu.VMEM),) * 2,
        scratch_shapes=[
            pltpu.VMEM((2, 4, B, B), jnp.bfloat16),
            *buffers(16, 2),
            *buffers(16, 2),
            *buffers(8, 2),
            *buffers(4, 2),
            *buffers(16, 2),
            *buffers(16),
            *buffers(16),
            *buffers(16),
            *buffers(16),
            *buffers(16),
            pltpu.SMEM((16,), jnp.int32),
            pltpu.SMEM((16,), jnp.int32),
            pltpu.SemaphoreType.DMA((2,)),
            *semaphores(2, 4),
            *semaphores(2, 2),
            *semaphores(2, 16),
            *semaphores(2, 4),
            *semaphores(2, 16),
            *semaphores(2, 16),
            pltpu.SemaphoreType.REGULAR,
        ],
        compiler_params=pltpu.CompilerParams(
            collective_id=0, has_side_effects=True, vmem_limit_bytes=52 * 1024 * 1024
        ),
        cost_estimate=pl.CostEstimate(flops=4 * 10**9, bytes_accessed=8 * 10**6, transcendentals=0),
        name="route",
    )(table, grads)


def split(a):
    high = a.astype(jnp.bfloat16)
    return high, (a - high.astype(jnp.float32)).astype(jnp.bfloat16)


def halves(matrix):
    return {place: split(quarter) for place, quarter in matrix.items()}


def product(a, b):
    out = {}
    for r, c in ((0, 0), (0, 1), (1, 1)):
        left, right = [], []
        for k in range(2):
            left += [a[r, k][0], a[r, k][0], a[r, k][1]]
            right += [b[k, c][0], b[k, c][1], b[k, c][0]]
        out[r, c] = jnp.dot(
            jnp.concatenate(left, axis=1), jnp.concatenate(right, axis=0), preferred_element_type=jnp.float32
        )
    out[1, 0] = out[0, 1].T
    return out


def newton(tri0, tri1, old, stats, roots):
    def blend(i, j, block):
        rows, cols = slice(i * T, (i + 1) * T), slice(j * T, (j + 1) * T)
        stats[rows, cols] = BETA * old[rows, cols] + (1.0 - BETA) * block

    mask = low_left()
    kept = []
    for tri, n, (i, j) in [(tri, n, p) for tri, ps in zip((tri0, tri1), PARTS) for n, p in enumerate(ps)]:
        block = tri[:, n].reshape(T, T)
        if i == j:
            kept.append(block)
            blend(i, i, jnp.where(mask, block.T, block))
        else:
            blend(i, j, block)
            blend(j, i, block.T)
    first, second, third = kept
    left = lax.broadcasted_iota(jnp.int32, (T // 2, T), 1) < T // 2
    top = jnp.where(left, first[T // 2:], turned(second[T // 2:]))
    corner = jnp.concatenate([top, turned(third[T // 2:])], axis=0)
    blend(3, 3, jnp.where(mask, corner.T, corner))

    scale = 2.5 / jnp.sqrt(jnp.sum(stats[...] * stats[...], keepdims=True) + 1e-06)
    eye = lax.broadcasted_iota(jnp.int32, (H, H), 0) == lax.broadcasted_iota(jnp.int32, (H, H), 1)

    def factor_of(matrix):
        return {
            (r, c): (jnp.where(eye, 1.25, 0.0) if r == c else 0.0) - 0.25 * quarter
            for (r, c), quarter in matrix.items()
        }

    moving = {
        (r, c): scale * stats[r * H:(r + 1) * H, c * H:(c + 1) * H] for r in range(2) for c in range(2)
    }
    root = factor_of(moving)
    factor = halves(root)
    for sweep in range(1, ITERS):
        square = halves(product(factor, factor))
        fourth = halves(product(square, square))
        moving = product(fourth, halves(moving))
        factor = halves(factor_of(moving))
        root = product(halves(root), factor)
    post = jnp.sqrt(jnp.sqrt(scale))
    for (r, c), quarter in root.items():
        roots[r * H:(r + 1) * H, c * H:(c + 1) * H] = post * quarter


def finished(tri0, tri1, old):
    whole = pl.BlockSpec(memory_space=pltpu.VMEM)
    return pl.pallas_call(
        newton,
        out_shape=(jax.ShapeDtypeStruct((B, B), jnp.float32),) * 2,
        in_specs=[whole] * 3,
        out_specs=(whole, whole),
        compiler_params=pltpu.CompilerParams(vmem_limit_bytes=48 * 1024 * 1024),
        cost_estimate=pl.CostEstimate(flops=13 * 10**9, bytes_accessed=4 * 10**6, transcendentals=0),
        name="newton",
    )(tri0, tri1, old)


def local(gradients, old_stats, owner_table):
    tri0, tri1 = routed(owner_table, gradients[0])
    stats, roots = finished(tri0, tri1, old_stats[0, 0])
    return (stats[None, None], roots[None, None])


def solution(mesh):
    placed = (P("dp", "factor", None, None), P("dp", "factor", None, None), P())
    return jax.shard_map(
        local,
        mesh=mesh,
        in_specs=placed,
        out_specs=(P("dp", "factor", None, None), P("dp", "factor", None, None)),
        check_vma=False,
    )
```

time: 121 us -> 116 us (0.959)
  Pallas kernels: 120 us -> 114 us
    pallas_call x1, Pallas kernels: 108 us -> 102 us  [routed(): pl.pallas_call(route, out_shape=tuple((jax.ShapeDtypeStruct((16,) + tile,...]
where the time goes in v5:
time: 116 us; the launch traced here: 115 us
  Pallas kernels  114 us (98%)
    pallas_call x1, Pallas kernels, routed(): pl.pallas_call(route, out_shape=tuple((jax.ShapeDtypeStruct((16,) + tile,...  102 us
    pallas_call x1, Pallas kernels, finished(): pl.pallas_call(newton, out_shape=(jax.ShapeDtypeStruct((B, B), jnp.float3...  11.7 us

profile of v5, /device:TPU:1, one launch (start us, length us, event | category | flops | bytes accessed | tf_op | source)
XLA Modules:
  0.0 115.5 jit_solution(17566411187736929877)
XLA Ops:
  0.6 0.0 copy-start.1
  0.6 0.7 copy-done.1
  1.3 0.0 copy-start
  1.3 102.4 %route.1 = (f32[16,4,8,128]{3,2,1,0:T(8,128)S(1)}, f32[16,5,8,128]{3,2,1,0:T(8,128)S(1)}) custom-call(s32[16,16]{1,0:T(8,128)S(1)} %copy-done.1, bf16[8,512,512]{2,1,0:T(8,128)(2,1)} %bitcast.5), custom_call_target="tpu_custom_call" | custom-call | flops 4000000000 | bytes 8000000 | tf_op jit(solution)/shard_map/route/pallas_call | solution.py:269
  103.7 0.0 copy-done
  103.7 11.7 %newton.1 = (f32[512,512]{1,0:T(8,128)}, f32[512,512]{1,0:T(8,128)}) custom-call(f32[16,4,8,128]{3,2,1,0:T(8,128)S(1)} %get-tuple-element.6.tri0, f32[16,5,8,128]{3,2,1,0:T(8,128)S(1)} %get-tuple-element.7.tri1, f32[512,512]{1,0:T(8,128)S(1)} %bitcast.4), custom_call_target="tpu_custom_call" | custom-call | flops 12999999488 | bytes 4000000 | tf_op jit(solution)/shard_map/newton/pallas_call | solution.py:379
Async XLA Ops:
  0.6 0.7 copy-start.1
  1.3 102.4 %copy-start = (f32[1,1,512,512]{3,2,1,0:T(8,128)S(1)}, f32[1,1,512,512]{3,2,1,0:T(8,128)}, u32[]{:S(2)}) copy-start(f32[1,1,512,512]{3,2,1,0:T(8,128)} %param.4) | copy-start | bytes 3145732

commit v6 on v5

--- a/solution.py
+++ b/solution.py
@@ -30,14 +30,14 @@
 
 
 def route(table, grads, out0, out1, xg, part0, part1, last0, last1, r10, r11, r20, r21, r30, r31, xt0, xt1, fs0, fs1, fr0, fr1,
-          ds0, ds1, dr0, dr1, items, columns, own_sem, xs, xr, zs, zr, ws, wr, ts, tr, as_, ar, bs, br, turn):
+          ds0, ds1, dr0, dr1, items, columns, own_sem, xs, xr, zs, zr, ws, wr, ts, tr, as_, ar, bs, br, turn, ready):
     r1, r2 = (r10, r11), (r20, r21)
     part, last, r3, xt = (part0, part1), (last0, last1), (r30, r31), (xt0, xt1)
     fs, fr, ds, dr, out = (fs0, fs1), (fr0, fr1), (ds0, ds1), (dr0, dr1), (out0, out1)
     d = lax.axis_index("dp")
     f = lax.axis_index("factor")
     x, zl = d // 4, d % 4
-    zh, core = f // 8, f % 2
+    zh, y, core = f // 8, (f // 2) % 4, f % 2
     q = zl + zh * (3 - 2 * zl)
     b0, b1 = q % 2, q // 2
     home = b0 * 8 + b1 * 4
@@ -59,13 +59,20 @@
     def d_peer(e):
         return {"dp": e, "factor": f}
 
+    partner = {"dp": d, "factor": f + 1 - 2 * core}
+    along_z = [{"dp": dp_at(x, (q + k) % 4, zh), "factor": f} for k in range(1, 4)]
+    along_y = [{"dp": d, "factor": zh * 8 + ((y + k) % 4) * 2 + core} for k in range(1, 4)]
+    across = {"dp": dp_at(x, q, 1 - zh), "factor": (1 - zh) * 8 + y * 2 + core}
     barrier = pltpu.get_barrier_semaphore()
-    for k in range(1, 16):
-        pl.semaphore_signal(barrier, inc=1, device_id=d_peer((d + k) % 16), device_id_type=MESH)
-        pl.semaphore_signal(barrier, inc=1, device_id=f_peer((f + k) % 16), device_id_type=MESH)
+    for peer in [x_peer(k) for k in range(1, 4)] + [partner] + along_z + along_y + [across]:
+        pl.semaphore_signal(barrier, inc=1, device_id=peer, device_id_type=MESH)
     own = [pltpu.make_async_copy(grads.at[2 * x + c], xg.at[c, 0], own_sem.at[c]) for c in range(2)]
     for copy in own:
         copy.start()
+
+    others_d = [dp_at((x + k // 2) % 4, (1 - b1) * 2 + k % 2, zh) for k in range(8)]
+    others_d += [dp_at((x + k // 2) % 4, b1 * 2 + (b0 + k) % 2, zh) for k in range(1, 8)]
+    others_f = [(1 - zh) * 8 + (f + k) % 8 for k in range(8)] + [zh * 8 + (f + k) % 8 for k in range(1, 8)]
 
     def find_column(e, carry):
         def scan(c, found):
@@ -75,7 +82,7 @@
         columns[e] = lax.fori_loop(0, 16, scan, jnp.int32(0))
         return carry
 
-    pl.semaphore_wait(barrier, 30)
+    pl.semaphore_wait(barrier, 11)
 
     def x_copy(c, k):
         return pltpu.make_async_remote_copy(
@@ -161,7 +168,6 @@
                     kept[h][:, side, n] = block.reshape(16, 8, T)
 
     order = (2, 1, 3)
-    partner = {"dp": d, "factor": f + 1 - 2 * core}
 
     def send_x(c):
         for k in order:
@@ -183,6 +189,10 @@
             pick = jnp.where(lax.shift_right_logical(table[f, j], 4) == g, j, pick)
         items[g] = pick
     lax.fori_loop(0, 16, find_column, 0)
+    for axis, peers in enumerate((along_z, along_y, [across])):
+        for peer in peers:
+            pl.semaphore_signal(ready.at[axis], inc=1, device_id=peer, device_id_type=MESH)
+        pl.semaphore_wait(ready.at[axis], len(peers))
     x_copy(0, 1).wait_send()
     pl.semaphore_signal(turn, inc=1, device_id=partner, device_id_type=MESH)
 
@@ -213,34 +223,32 @@
     for h in range(2):
         for side in range(2):
             gram(1, h, side)
-        for k in range(1, 16):
-            w_copy(h, (d + k) % 16).start()
+        for e in others_d:
+            w_copy(h, e).start()
         r3[h][d] = last[h][piece]
     for h in range(2):
         for k in order:
             t_copy(h, k).wait_recv()
     for h in range(2):
-        for k in range(1, 16):
-            w_landed(h, (d + k) % 16).wait_recv()
+        for e in others_d:
+            w_landed(h, e).wait_recv()
         for i in range(4):
             here = r3[h][4 * i:4 * i + 4]
             xt[h][4 * i + 2:4 * i + 4] = (here[0] + here[1]) + (here[2] + here[3])
-        for k in range(1, 16):
-            g = (f + k) % 16
+        for g in others_f:
             fs[h][g] = xt[h][items[g]]
             a_copy(h, g).start()
         fr[h][f] = xt[h][items[f]]
     for h in range(2):
-        for k in range(1, 16):
-            a_landed(h, (f + k) % 16).wait_recv()
-        for k in range(1, 16):
-            e = (d + k) % 16
+        for g in others_f:
+            a_landed(h, g).wait_recv()
+        for e in others_d:
             ds[h][e] = fr[h][columns[e]]
             b_copy(h, e).start()
         dr[h][piece] = fr[h][columns[d]]
     for h in range(2):
-        for k in range(1, 16):
-            b_landed(h, (d + k) % 16).wait_recv()
+        for e in others_d:
+            b_landed(h, e).wait_recv()
         out[h][...] = dr[h][...]
 
     for c in range(2):
@@ -251,10 +259,11 @@
             z_copy(h, step).wait_send()
         for k in order:
             t_copy(h, k).wait_send()
-        for k in range(1, 16):
-            w_copy(h, (d + k) % 16).wait_send()
-            a_copy(h, (f + k) % 16).wait_send()
-            b_copy(h, (d + k) % 16).wait_send()
+        for e in others_d:
+            w_copy(h, e).wait_send()
+            b_copy(h, e).wait_send()
+        for g in others_f:
+            a_copy(h, g).wait_send()
 
 
 def routed(table, grads):
@@ -296,6 +305,7 @@
             *semaphores(2, 16),
             *semaphores(2, 16),
             pltpu.SemaphoreType.REGULAR,
+            pltpu.SemaphoreType.REGULAR((3,)),
         ],
         compiler_params=pltpu.CompilerParams(
             collective_id=0, has_side_effects=True, vmem_limit_bytes=52 * 1024 * 1024

time: 116 us -> 116 us (level)
  no operation moved by 1% of the time
where the time goes in v6:
time: 116 us; the launch traced here: 115 us
  Pallas kernels  114 us (98%)
    pallas_call x1, Pallas kernels, routed(): pl.pallas_call(route, out_shape=tuple((jax.ShapeDtypeStruct((16,) + tile,...  102 us
    pallas_call x1, Pallas kernels, finished(): pl.pallas_call(newton, out_shape=(jax.ShapeDtypeStruct((B, B), jnp.float3...  11.7 us

profile of v6, /device:TPU:1, one launch (start us, length us, event | category | flops | bytes accessed | tf_op | source)
XLA Modules:
  0.0 115.0 jit_solution(15617283940012264547)
XLA Ops:
  0.6 0.0 copy-start.1
  0.6 0.7 copy-done.1
  1.3 0.0 copy-start
  1.3 101.9 %route.1 = (f32[16,4,8,128]{3,2,1,0:T(8,128)S(1)}, f32[16,5,8,128]{3,2,1,0:T(8,128)S(1)}) custom-call(s32[16,16]{1,0:T(8,128)S(1)} %copy-done.1, bf16[8,512,512]{2,1,0:T(8,128)(2,1)} %bitcast.5), custom_call_target="tpu_custom_call" | custom-call | flops 4000000000 | bytes 8000000 | tf_op jit(solution)/shard_map/route/pallas_call | solution.py:278
  103.2 0.0 copy-done
  103.2 11.7 %newton.1 = (f32[512,512]{1,0:T(8,128)}, f32[512,512]{1,0:T(8,128)}) custom-call(f32[16,4,8,128]{3,2,1,0:T(8,128)S(1)} %get-tuple-element.6.tri0, f32[16,5,8,128]{3,2,1,0:T(8,128)S(1)} %get-tuple-element.7.tri1, f32[512,512]{1,0:T(8,128)S(1)} %bitcast.4), custom_call_target="tpu_custom_call" | custom-call | flops 12999999488 | bytes 4000000 | tf_op jit(solution)/shard_map/newton/pallas_call | solution.py:389
Async XLA Ops:
  0.6 0.7 copy-start.1
  1.3 101.9 %copy-start = (f32[1,1,512,512]{3,2,1,0:T(8,128)S(1)}, f32[1,1,512,512]{3,2,1,0:T(8,128)}, u32[]{:S(2)}) copy-start(f32[1,1,512,512]{3,2,1,0:T(8,128)} %param.4) | copy-start | bytes 3145732

commit v7 on v6

--- a/solution.py
+++ b/solution.py
@@ -29,29 +29,25 @@
     return jnp.concatenate([block[:, T // 2:], block[:, :T // 2]], axis=1)
 
 
-def route(table, grads, out0, out1, xg, part0, part1, last0, last1, r10, r11, r20, r21, r30, r31, xt0, xt1, fs0, fs1, fr0, fr1,
-          ds0, ds1, dr0, dr1, items, columns, own_sem, xs, xr, zs, zr, ws, wr, ts, tr, as_, ar, bs, br, turn, ready):
-    r1, r2 = (r10, r11), (r20, r21)
-    part, last, r3, xt = (part0, part1), (last0, last1), (r30, r31), (xt0, xt1)
-    fs, fr, ds, dr, out = (fs0, fs1), (fr0, fr1), (ds0, ds1), (dr0, dr1), (out0, out1)
+def route(table, grads, out0, out1, xg, *refs):
+    pairs = [(refs[2 * i], refs[2 * i + 1]) for i in range(11)]
+    part, r1, r3 = ([pairs[2 * i], pairs[2 * i + 1]] for i in range(3))
+    xt, fs, fr, ds, dr = pairs[6:]
+    items, columns, own_sem, xs, xr, zs, zr, ws, wr, as_, ar, bs, br, turn, ready = refs[22:]
+    out = (out0, out1)
     d = lax.axis_index("dp")
     f = lax.axis_index("factor")
     x, zl = d // 4, d % 4
     zh, y, core = f // 8, (f // 2) % 4, f % 2
     q = zl + zh * (3 - 2 * zl)
     b0, b1 = q % 2, q // 2
-    home = b0 * 8 + b1 * 4
-    piece = home + x
+    piece = b0 * 8 + b1 * 4 + x
 
     def dp_at(x_, q_, zh_):
         return x_ * 4 + q_ + zh_ * (3 - 2 * q_)
 
     def x_peer(k):
         return {"dp": dp_at((x + k) % 4, q, zh), "factor": f}
-
-    def z_peer(step):
-        flip = q + 1 - 2 * b0 if step == 0 else q + 2 - 4 * b1
-        return {"dp": dp_at(x, flip, zh), "factor": f}
 
     def f_peer(g):
         return {"dp": dp_at(x, q, g // 8), "factor": g}
@@ -84,39 +80,38 @@
 
     pl.semaphore_wait(barrier, 11)
 
-    def x_copy(c, k):
-        return pltpu.make_async_remote_copy(
-            src_ref=grads.at[2 * ((x + k) % 4) + c], dst_ref=xg.at[c, k],
-            send_sem=xs.at[c, k], recv_sem=xr.at[c, k], device_id=x_peer(k), device_id_type=MESH)
-
-    def z_copy(h, step):
-        if step == 0:
-            src, dst = part[h].at[pl.ds((1 - b0) * 8, 8)], r1[h]
-        else:
-            src, dst = part[h].at[pl.ds(b0 * 8 + (1 - b1) * 4, 4)], r2[h]
-        return pltpu.make_async_remote_copy(
-            src_ref=src, dst_ref=dst, send_sem=zs.at[h, step], recv_sem=zr.at[h, step],
-            device_id=z_peer(step), device_id_type=MESH)
-
-    def t_copy(h, k):
-        return pltpu.make_async_remote_copy(
-            src_ref=part[h].at[home + (x + k) % 4], dst_ref=xt[h].at[pl.ds(4 * x, 2)],
-            send_sem=ts.at[h, k], recv_sem=tr.at[h, k], device_id=x_peer(k), device_id_type=MESH)
+    def x_copy(c, k, half):
+        rows = pl.ds(half * H, H)
+        return pltpu.make_async_remote_copy(
+            src_ref=grads.at[2 * ((x + k) % 4) + c, rows], dst_ref=xg.at[c, k, rows],
+            send_sem=xs.at[c, k, half], recv_sem=xr.at[c, k, half], device_id=x_peer(k), device_id_type=MESH)
+
+    def z_copy(c, h):
+        return pltpu.make_async_remote_copy(
+            src_ref=part[c][h].at[pl.ds((1 - b0) * 8, 8)], dst_ref=r1[c][h],
+            send_sem=zs.at[c, h], recv_sem=zr.at[c, h],
+            device_id={"dp": dp_at(x, q + 1 - 2 * b0, zh), "factor": f}, device_id_type=MESH)
+
+    places = [((x + k) % 4, 1 - b1) for k in range(4)] + [((x + k) % 4, b1) for k in range(1, 4)]
+
+    def w_copy(c, h, to):
+        slot = to[0] * 2 + to[1]
+        return pltpu.make_async_remote_copy(
+            src_ref=part[c][h].at[b0 * 8 + to[1] * 4 + to[0]], dst_ref=r3[c][h].at[x * 2 + b1],
+            send_sem=ws.at[c, h, slot], recv_sem=wr.at[c, h, x * 2 + b1],
+            device_id={"dp": dp_at(to[0], b0 + 2 * to[1], zh), "factor": f}, device_id_type=MESH)
+
+    def w_landed(c, h, to):
+        slot = to[0] * 2 + to[1]
+        return pltpu.make_async_remote_copy(
+            src_ref=part[c][h].at[b0 * 8 + to[1] * 4 + to[0]], dst_ref=r3[c][h].at[slot],
+            send_sem=ws.at[c, h, slot], recv_sem=wr.at[c, h, slot],
+            device_id={"dp": dp_at(to[0], b0 + 2 * to[1], zh), "factor": f}, device_id_type=MESH)
 
     def piece_of(e):
         e_x, e_zl = e // 4, e % 4
         e_q = e_zl + zh * (3 - 2 * e_zl)
         return (e_q % 2) * 8 + (e_q // 2) * 4 + e_x
-
-    def w_copy(h, e):
-        return pltpu.make_async_remote_copy(
-            src_ref=last[h].at[piece_of(e)], dst_ref=r3[h].at[d], send_sem=ws.at[h, e], recv_sem=wr.at[h, d],
-            device_id=d_peer(e), device_id_type=MESH)
-
-    def w_landed(h, e):
-        return pltpu.make_async_remote_copy(
-            src_ref=last[h].at[piece_of(e)], dst_ref=r3[h].at[e], send_sem=ws.at[h, e], recv_sem=wr.at[h, e],
-            device_id=d_peer(e), device_id_type=MESH)
 
     def a_copy(h, g):
         return pltpu.make_async_remote_copy(
@@ -164,19 +159,41 @@
                     block = total[i0:i0 + T, j0:j0 + T]
                     if i == j:
                         block = jnp.where(low_left(), corner_parts[i], block)
-                    kept = part if c == 0 else last
-                    kept[h][:, side, n] = block.reshape(16, 8, T)
+                    part[c][h][:, side, n] = block.reshape(16, 8, T)
 
     order = (2, 1, 3)
 
     def send_x(c):
+        for half in range(2):
+            for k in order:
+                x_copy(c, k, half).start()
+
+    def half_sent(c):
         for k in order:
-            x_copy(c, k).start()
+            x_copy(c, k, 0).wait_send()
 
     def arrive(c):
         own[c].wait()
-        for k in order:
-            x_copy(c, k).wait_recv()
+        for half in range(2):
+            for k in order:
+                x_copy(c, k, half).wait_recv()
+        for h in range(2):
+            for side in range(2):
+                gram(c, h, side)
+            z_copy(c, h).start()
+
+    def pass_on(c, h):
+        z_copy(c, h).wait_recv()
+        part[c][h][pl.ds(b0 * 8, 8)] += r1[c][h][...]
+        for to in places:
+            w_copy(c, h, to).start()
+        r3[c][h][x * 2 + b1] = part[c][h][piece]
+
+    def settle(c, h):
+        for to in places:
+            w_landed(c, h, to).wait_recv()
+        for i in range(4):
+            xt[h][4 * i + 2 * c:4 * i + 2 * c + 2] = r3[c][h][2 * i] + r3[c][h][2 * i + 1]
 
     @pl.when(core == 1)
     def _():
@@ -188,32 +205,20 @@
         for j in range(16):
             pick = jnp.where(lax.shift_right_logical(table[f, j], 4) == g, j, pick)
         items[g] = pick
+    half_sent(0)
+    pl.semaphore_signal(turn, inc=1, device_id=partner, device_id_type=MESH)
     lax.fori_loop(0, 16, find_column, 0)
     for axis, peers in enumerate((along_z, along_y, [across])):
         for peer in peers:
             pl.semaphore_signal(ready.at[axis], inc=1, device_id=peer, device_id_type=MESH)
         pl.semaphore_wait(ready.at[axis], len(peers))
-    x_copy(0, 1).wait_send()
-    pl.semaphore_signal(turn, inc=1, device_id=partner, device_id_type=MESH)
 
     arrive(0)
-    for h in range(2):
-        for side in range(2):
-            gram(0, h, side)
-        z_copy(h, 0).start()
-    for h in range(2):
-        z_copy(h, 0).wait_recv()
-        part[h][pl.ds(b0 * 8, 8)] += r1[h][...]
-        z_copy(h, 1).start()
     pl.semaphore_wait(turn, 1)
     send_x(1)
     for h in range(2):
-        z_copy(h, 1).wait_recv()
-        part[h][pl.ds(home, 4)] += r2[h][...]
-        for k in order:
-            t_copy(h, k).start()
-        xt[h][pl.ds(4 * x, 2)] = part[h][piece]
-    x_copy(1, 1).wait_send()
+        pass_on(0, h)
+    half_sent(1)
 
     @pl.when(core == 0)
     def _():
@@ -221,20 +226,11 @@
 
     arrive(1)
     for h in range(2):
-        for side in range(2):
-            gram(1, h, side)
-        for e in others_d:
-            w_copy(h, e).start()
-        r3[h][d] = last[h][piece]
-    for h in range(2):
-        for k in order:
-            t_copy(h, k).wait_recv()
-    for h in range(2):
-        for e in others_d:
-            w_landed(h, e).wait_recv()
-        for i in range(4):
-            here = r3[h][4 * i:4 * i + 4]
-            xt[h][4 * i + 2:4 * i + 4] = (here[0] + here[1]) + (here[2] + here[3])
+        settle(0, h)
+    for h in range(2):
+        pass_on(1, h)
+    for h in range(2):
+        settle(1, h)
         for g in others_f:
             fs[h][g] = xt[h][items[g]]
             a_copy(h, g).start()
@@ -252,15 +248,14 @@
         out[h][...] = dr[h][...]
 
     for c in range(2):
-        for k in (2, 3):
-            x_copy(c, k).wait_send()
-    for h in range(2):
-        for step in range(2):
-            z_copy(h, step).wait_send()
         for k in order:
-            t_copy(h, k).wait_send()
+            x_copy(c, k, 1).wait_send()
+        for h in range(2):
+            z_copy(c, h).wait_send()
+            for to in places:
+                w_copy(c, h, to).wait_send()
+    for h in range(2):
         for e in others_d:
-            w_copy(h, e).wait_send()
             b_copy(h, e).wait_send()
         for g in others_f:
             a_copy(h, g).wait_send()
@@ -285,23 +280,16 @@
         out_specs=(pl.BlockSpec(memory_space=pltpu.VMEM),) * 2,
         scratch_shapes=[
             pltpu.VMEM((2, 4, B, B), jnp.bfloat16),
-            *buffers(16, 2),
-            *buffers(16, 2),
-            *buffers(8, 2),
-            *buffers(4, 2),
-            *buffers(16, 2),
-            *buffers(16),
-            *buffers(16),
-            *buffers(16),
-            *buffers(16),
-            *buffers(16),
+            *buffers(16, 2) * 2,
+            *buffers(8, 2) * 2,
+            *buffers(8, 2) * 2,
+            *buffers(16) * 5,
             pltpu.SMEM((16,), jnp.int32),
             pltpu.SMEM((16,), jnp.int32),
             pltpu.SemaphoreType.DMA((2,)),
-            *semaphores(2, 4),
+            *semaphores(2, 4, 2),
             *semaphores(2, 2),
-            *semaphores(2, 16),
-            *semaphores(2, 4),
+            *semaphores(2, 2, 8),
             *semaphores(2, 16),
             *semaphores(2, 16),
             pltpu.SemaphoreType.REGULAR,

time: 116 us -> 117 us (level)
    pallas_call x1, Pallas kernels: 102 us -> 104 us  [routed(): pl.pallas_call(route, out_shape=tuple((jax.ShapeDtypeStruct((16,) + tile,...]
where the time goes in v7:
time: 117 us
  Pallas kernels  115 us (98%)
    pallas_call x1, Pallas kernels, routed(): pl.pallas_call(route, out_shape=tuple((jax.ShapeDtypeStruct((16,) + tile,...  104 us
    pallas_call x1, Pallas kernels, finished(): pl.pallas_call(newton, out_shape=(jax.ShapeDtypeStruct((B, B), jnp.float3...  11.7 us

profile of v7, /device:TPU:1, one launch (start us, length us, event | category | flops | bytes accessed | tf_op | source)
XLA Modules:
  0.0 116.7 jit_solution(14905358869245853902)
XLA Ops:
  0.6 0.0 copy-start.1
  0.6 0.7 copy-done.1
  1.3 0.0 copy-start
  1.3 103.6 %route.1 = (f32[16,4,8,128]{3,2,1,0:T(8,128)S(1)}, f32[16,5,8,128]{3,2,1,0:T(8,128)S(1)}) custom-call(s32[16,16]{1,0:T(8,128)S(1)} %copy-done.1, bf16[8,512,512]{2,1,0:T(8,128)(2,1)} %bitcast.5), custom_call_target="tpu_custom_call" | custom-call | flops 4000000000 | bytes 8000000 | tf_op jit(solution)/shard_map/route/pallas_call | solution.py:273
  105.0 0.0 copy-done
  105.0 11.7 %newton.1 = (f32[512,512]{1,0:T(8,128)}, f32[512,512]{1,0:T(8,128)}) custom-call(f32[16,4,8,128]{3,2,1,0:T(8,128)S(1)} %get-tuple-element.6.tri0, f32[16,5,8,128]{3,2,1,0:T(8,128)S(1)} %get-tuple-element.7.tri1, f32[512,512]{1,0:T(8,128)S(1)} %bitcast.4), custom_call_target="tpu_custom_call" | custom-call | flops 12999999488 | bytes 4000000 | tf_op jit(solution)/shard_map/newton/pallas_call | solution.py:377
Async XLA Ops:
  0.6 0.7 copy-start.1
  1.3 103.6 %copy-start = (f32[1,1,512,512]{3,2,1,0:T(8,128)S(1)}, f32[1,1,512,512]{3,2,1,0:T(8,128)}, u32[]{:S(2)}) copy-start(f32[1,1,512,512]{3,2,1,0:T(8,128)} %param.4) | copy-start | bytes 3145732

commit v8 on v7

--- a/solution.py
+++ b/solution.py
@@ -66,9 +66,8 @@
     for copy in own:
         copy.start()
 
-    others_d = [dp_at((x + k // 2) % 4, (1 - b1) * 2 + k % 2, zh) for k in range(8)]
-    others_d += [dp_at((x + k // 2) % 4, b1 * 2 + (b0 + k) % 2, zh) for k in range(1, 8)]
-    others_f = [(1 - zh) * 8 + (f + k) % 8 for k in range(8)] + [zh * 8 + (f + k) % 8 for k in range(1, 8)]
+    others_d = [(d + k) % 16 for k in range(1, 16)]
+    others_f = [(f + k) % 16 for k in range(1, 16)]
 
     def find_column(e, carry):
         def scan(c, found):
@@ -92,7 +91,7 @@
             send_sem=zs.at[c, h], recv_sem=zr.at[c, h],
             device_id={"dp": dp_at(x, q + 1 - 2 * b0, zh), "factor": f}, device_id_type=MESH)
 
-    places = [((x + k) % 4, 1 - b1) for k in range(4)] + [((x + k) % 4, b1) for k in range(1, 4)]
+    places = [((x + k) % 4, up) for k in range(1, 4) for up in (1 - b1, b1)] + [(x, 1 - b1)]
 
     def w_copy(c, h, to):
         slot = to[0] * 2 + to[1]

time: 117 us -> 115 us (0.983)
  Pallas kernels: 115 us -> 113 us
    pallas_call x1, Pallas kernels: 104 us -> 101 us  [routed(): pl.pallas_call(route, out_shape=tuple((jax.ShapeDtypeStruct((16,) + tile,...]
where the time goes in v8:
time: 115 us; the launch traced here: 114 us
  Pallas kernels  113 us (98%)
    pallas_call x1, Pallas kernels, routed(): pl.pallas_call(route, out_shape=tuple((jax.ShapeDtypeStruct((16,) + tile,...  101 us
    pallas_call x1, Pallas kernels, finished(): pl.pallas_call(newton, out_shape=(jax.ShapeDtypeStruct((B, B), jnp.float3...  11.7 us

profile of v8, /device:TPU:1, one launch (start us, length us, event | category | flops | bytes accessed | tf_op | source)
XLA Modules:
  0.0 114.3 jit_solution(15630302156559059274)
XLA Ops:
  0.6 0.0 copy-start.1
  0.6 0.7 copy-done.1
  1.3 0.0 copy-start
  1.3 101.2 %route.1 = (f32[16,4,8,128]{3,2,1,0:T(8,128)S(1)}, f32[16,5,8,128]{3,2,1,0:T(8,128)S(1)}) custom-call(s32[16,16]{1,0:T(8,128)S(1)} %copy-done.1, bf16[8,512,512]{2,1,0:T(8,128)(2,1)} %bitcast.5), custom_call_target="tpu_custom_call" | custom-call | flops 4000000000 | bytes 8000000 | tf_op jit(solution)/shard_map/route/pallas_call | solution.py:272
  102.5 0.0 copy-done
  102.5 11.7 %newton.1 = (f32[512,512]{1,0:T(8,128)}, f32[512,512]{1,0:T(8,128)}) custom-call(f32[16,4,8,128]{3,2,1,0:T(8,128)S(1)} %get-tuple-element.6.tri0, f32[16,5,8,128]{3,2,1,0:T(8,128)S(1)} %get-tuple-element.7.tri1, f32[512,512]{1,0:T(8,128)S(1)} %bitcast.4), custom_call_target="tpu_custom_call" | custom-call | flops 12999999488 | bytes 4000000 | tf_op jit(solution)/shard_map/newton/pallas_call | solution.py:376
Async XLA Ops:
  0.6 0.7 copy-start.1
  1.3 101.2 %copy-start = (f32[1,1,512,512]{3,2,1,0:T(8,128)S(1)}, f32[1,1,512,512]{3,2,1,0:T(8,128)}, u32[]{:S(2)}) copy-start(f32[1,1,512,512]{3,2,1,0:T(8,128)} %param.4) | copy-start | bytes 3145732

commit v9 on v8

--- a/solution.py
+++ b/solution.py
@@ -205,7 +205,7 @@
             pick = jnp.where(lax.shift_right_logical(table[f, j], 4) == g, j, pick)
         items[g] = pick
     half_sent(0)
-    pl.semaphore_signal(turn, inc=1, device_id=partner, device_id_type=MESH)
+    send_x(1)
     lax.fori_loop(0, 16, find_column, 0)
     for axis, peers in enumerate((along_z, along_y, [across])):
         for peer in peers:
@@ -213,16 +213,14 @@
         pl.semaphore_wait(ready.at[axis], len(peers))
 
     arrive(0)
-    pl.semaphore_wait(turn, 1)
-    send_x(1)
-    for h in range(2):
-        pass_on(0, h)
     half_sent(1)
 
     @pl.when(core == 0)
     def _():
         pl.semaphore_signal(turn, inc=1, device_id=partner, device_id_type=MESH)
 
+    for h in range(2):
+        pass_on(0, h)
     arrive(1)
     for h in range(2):
         settle(0, h)

time: 115 us -> 114 us (level)
  no operation moved by 1% of the time
where the time goes in v9:
time: 114 us
  Pallas kernels  113 us (99%)
    pallas_call x1, Pallas kernels, routed(): pl.pallas_call(route, out_shape=tuple((jax.ShapeDtypeStruct((16,) + tile,...  101 us
    pallas_call x1, Pallas kernels, finished(): pl.pallas_call(newton, out_shape=(jax.ShapeDtypeStruct((B, B), jnp.float3...  11.7 us

profile of v9, /device:TPU:1, one launch (start us, length us, event | category | flops | bytes accessed | tf_op | source)
XLA Modules:
  0.0 114.0 jit_solution(1248578544477476536)
XLA Ops:
  0.6 0.0 copy-start.1
  0.6 0.7 copy-done.1
  1.3 0.0 copy-start
  1.3 101.0 %route.1 = (f32[16,4,8,128]{3,2,1,0:T(8,128)S(1)}, f32[16,5,8,128]{3,2,1,0:T(8,128)S(1)}) custom-call(s32[16,16]{1,0:T(8,128)S(1)} %copy-done.1, bf16[8,512,512]{2,1,0:T(8,128)(2,1)} %bitcast.5), custom_call_target="tpu_custom_call" | custom-call | flops 4000000000 | bytes 8000000 | tf_op jit(solution)/shard_map/route/pallas_call | solution.py:270
  102.3 0.0 copy-done
  102.3 11.7 %newton.1 = (f32[512,512]{1,0:T(8,128)}, f32[512,512]{1,0:T(8,128)}) custom-call(f32[16,4,8,128]{3,2,1,0:T(8,128)S(1)} %get-tuple-element.6.tri0, f32[16,5,8,128]{3,2,1,0:T(8,128)S(1)} %get-tuple-element.7.tri1, f32[512,512]{1,0:T(8,128)S(1)} %bitcast.4), custom_call_target="tpu_custom_call" | custom-call | flops 12999999488 | bytes 4000000 | tf_op jit(solution)/shard_map/newton/pallas_call | solution.py:374
Async XLA Ops:
  0.6 0.7 copy-start.1
  1.3 101.0 %copy-start = (f32[1,1,512,512]{3,2,1,0:T(8,128)S(1)}, f32[1,1,512,512]{3,2,1,0:T(8,128)}, u32[]{:S(2)}) copy-start(f32[1,1,512,512]{3,2,1,0:T(8,128)} %param.4) | copy-start | bytes 3145732

commit v10 on v9

--- a/solution.py
+++ b/solution.py
@@ -223,10 +223,9 @@
         pass_on(0, h)
     arrive(1)
     for h in range(2):
+        pass_on(1, h)
+    for h in range(2):
         settle(0, h)
-    for h in range(2):
-        pass_on(1, h)
-    for h in range(2):
         settle(1, h)
         for g in others_f:
             fs[h][g] = xt[h][items[g]]

time: 114 us -> 114 us (level)
  no operation moved by 1% of the time
where the time goes in v10:
time: 114 us
  Pallas kernels  113 us (99%)
    pallas_call x1, Pallas kernels, routed(): pl.pallas_call(route, out_shape=tuple((jax.ShapeDtypeStruct((16,) + tile,...  101 us
    pallas_call x1, Pallas kernels, finished(): pl.pallas_call(newton, out_shape=(jax.ShapeDtypeStruct((B, B), jnp.float3...  11.7 us

profile of v10, /device:TPU:1, one launch (start us, length us, event | category | flops | bytes accessed | tf_op | source)
XLA Modules:
  0.0 114.0 jit_solution(7971093727595316556)
XLA Ops:
  0.6 0.0 copy-start.1
  0.6 0.7 copy-done.1
  1.3 0.0 copy-start
  1.3 101.0 %route.1 = (f32[16,4,8,128]{3,2,1,0:T(8,128)S(1)}, f32[16,5,8,128]{3,2,1,0:T(8,128)S(1)}) custom-call(s32[16,16]{1,0:T(8,128)S(1)} %copy-done.1, bf16[8,512,512]{2,1,0:T(8,128)(2,1)} %bitcast.5), custom_call_target="tpu_custom_call" | custom-call | flops 4000000000 | bytes 8000000 | tf_op jit(solution)/shard_map/route/pallas_call | solution.py:269
  102.3 0.0 copy-done
  102.3 11.7 %newton.1 = (f32[512,512]{1,0:T(8,128)}, f32[512,512]{1,0:T(8,128)}) custom-call(f32[16,4,8,128]{3,2,1,0:T(8,128)S(1)} %get-tuple-element.6.tri0, f32[16,5,8,128]{3,2,1,0:T(8,128)S(1)} %get-tuple-element.7.tri1, f32[512,512]{1,0:T(8,128)S(1)} %bitcast.4), custom_call_target="tpu_custom_call" | custom-call | flops 12999999488 | bytes 4000000 | tf_op jit(solution)/shard_map/newton/pallas_call | solution.py:373
Async XLA Ops:
  0.6 0.7 copy-start.1
  1.3 101.0 %copy-start = (f32[1,1,512,512]{3,2,1,0:T(8,128)S(1)}, f32[1,1,512,512]{3,2,1,0:T(8,128)}, u32[]{:S(2)}) copy-start(f32[1,1,512,512]{3,2,1,0:T(8,128)} %param.4) | copy-start | bytes 3145732

commit v11 on v8

--- a/solution.py
+++ b/solution.py
@@ -80,7 +80,7 @@
     pl.semaphore_wait(barrier, 11)
 
     def x_copy(c, k, half):
-        rows = pl.ds(half * H, H)
+        rows = pl.ds(0, 384) if half == 0 else pl.ds(384, 128)
         return pltpu.make_async_remote_copy(
             src_ref=grads.at[2 * ((x + k) % 4) + c, rows], dst_ref=xg.at[c, k, rows],
             send_sem=xs.at[c, k, half], recv_sem=xr.at[c, k, half], device_id=x_peer(k), device_id_type=MESH)
@@ -225,10 +225,9 @@
 
     arrive(1)
     for h in range(2):
+        pass_on(1, h)
+    for h in range(2):
         settle(0, h)
-    for h in range(2):
-        pass_on(1, h)
-    for h in range(2):
         settle(1, h)
         for g in others_f:
             fs[h][g] = xt[h][items[g]]

time: 115 us -> 117 us (1.017)
  Pallas kernels: 113 us -> 115 us
    pallas_call x1, Pallas kernels: 101 us -> 104 us  [routed(): pl.pallas_call(route, out_shape=tuple((jax.ShapeDtypeStruct((16,) + tile,...]
where the time goes in v11:
time: 117 us
  Pallas kernels  115 us (98%)
    pallas_call x1, Pallas kernels, routed(): pl.pallas_call(route, out_shape=tuple((jax.ShapeDtypeStruct((16,) + tile,...  104 us
    pallas_call x1, Pallas kernels, finished(): pl.pallas_call(newton, out_shape=(jax.ShapeDtypeStruct((B, B), jnp.float3...  11.7 us

profile of v11, /device:TPU:1, one launch (start us, length us, event | category | flops | bytes accessed | tf_op | source)
XLA Modules:
  0.0 116.8 jit_solution(15373285161041047085)
XLA Ops:
  0.6 0.0 copy-start.1
  0.6 0.7 copy-done.1
  1.3 0.0 copy-start
  1.3 103.7 %route.1 = (f32[16,4,8,128]{3,2,1,0:T(8,128)S(1)}, f32[16,5,8,128]{3,2,1,0:T(8,128)S(1)}) custom-call(s32[16,16]{1,0:T(8,128)S(1)} %copy-done.1, bf16[8,512,512]{2,1,0:T(8,128)(2,1)} %bitcast.5), custom_call_target="tpu_custom_call" | custom-call | flops 4000000000 | bytes 8000000 | tf_op jit(solution)/shard_map/route/pallas_call | solution.py:271
  105.1 0.0 copy-done
  105.1 11.7 %newton.1 = (f32[512,512]{1,0:T(8,128)}, f32[512,512]{1,0:T(8,128)}) custom-call(f32[16,4,8,128]{3,2,1,0:T(8,128)S(1)} %get-tuple-element.6.tri0, f32[16,5,8,128]{3,2,1,0:T(8,128)S(1)} %get-tuple-element.7.tri1, f32[512,512]{1,0:T(8,128)S(1)} %bitcast.4), custom_call_target="tpu_custom_call" | custom-call | flops 12999999488 | bytes 4000000 | tf_op jit(solution)/shard_map/newton/pallas_call | solution.py:375
Async XLA Ops:
  0.6 0.7 copy-start.1
  1.3 103.8 %copy-start = (f32[1,1,512,512]{3,2,1,0:T(8,128)S(1)}, f32[1,1,512,512]{3,2,1,0:T(8,128)}, u32[]{:S(2)}) copy-start(f32[1,1,512,512]{3,2,1,0:T(8,128)} %param.4) | copy-start | bytes 3145732

commit v12 on v10

--- a/solution.py
+++ b/solution.py
@@ -205,6 +205,8 @@
             pick = jnp.where(lax.shift_right_logical(table[f, j], 4) == g, j, pick)
         items[g] = pick
     half_sent(0)
+    for k in order:
+        x_copy(0, k, 1).wait_send()
     send_x(1)
     lax.fori_loop(0, 16, find_column, 0)
     for axis, peers in enumerate((along_z, along_y, [across])):
@@ -243,9 +245,9 @@
             b_landed(h, e).wait_recv()
         out[h][...] = dr[h][...]
 
+    for k in order:
+        x_copy(1, k, 1).wait_send()
     for c in range(2):
-        for k in order:
-            x_copy(c, k, 1).wait_send()
         for h in range(2):
             z_copy(c, h).wait_send()
             for to in places:

time: 114 us -> 119 us (1.044)
  Pallas kernels: 113 us -> 117 us
    pallas_call x1, Pallas kernels: 101 us -> 105 us  [routed(): pl.pallas_call(route, out_shape=tuple((jax.ShapeDtypeStruct((16,) + tile,...]
where the time goes in v12:
time: 119 us
  Pallas kernels  117 us (98%)
    pallas_call x1, Pallas kernels, routed(): pl.pallas_call(route, out_shape=tuple((jax.ShapeDtypeStruct((16,) + tile,...  105 us
    pallas_call x1, Pallas kernels, finished(): pl.pallas_call(newton, out_shape=(jax.ShapeDtypeStruct((B, B), jnp.float3...  11.7 us

profile of v12, /device:TPU:1, one launch (start us, length us, event | category | flops | bytes accessed | tf_op | source)
XLA Modules:
  0.0 118.5 jit_solution(17962012567832367368)
XLA Ops:
  0.6 0.0 copy-start.1
  0.6 0.7 copy-done.1
  1.3 0.0 copy-start
  1.3 105.4 %route.1 = (f32[16,4,8,128]{3,2,1,0:T(8,128)S(1)}, f32[16,5,8,128]{3,2,1,0:T(8,128)S(1)}) custom-call(s32[16,16]{1,0:T(8,128)S(1)} %copy-done.1, bf16[8,512,512]{2,1,0:T(8,128)(2,1)} %bitcast.5), custom_call_target="tpu_custom_call" | custom-call | flops 4000000000 | bytes 8000000 | tf_op jit(solution)/shard_map/route/pallas_call | solution.py:271
  106.8 0.0 copy-done
  106.8 11.7 %newton.1 = (f32[512,512]{1,0:T(8,128)}, f32[512,512]{1,0:T(8,128)}) custom-call(f32[16,4,8,128]{3,2,1,0:T(8,128)S(1)} %get-tuple-element.6.tri0, f32[16,5,8,128]{3,2,1,0:T(8,128)S(1)} %get-tuple-element.7.tri1, f32[512,512]{1,0:T(8,128)S(1)} %bitcast.4), custom_call_target="tpu_custom_call" | custom-call | flops 12999999488 | bytes 4000000 | tf_op jit(solution)/shard_map/newton/pallas_call | solution.py:375
Async XLA Ops:
  0.6 0.7 copy-start.1
  1.3 105.4 %copy-start = (f32[1,1,512,512]{3,2,1,0:T(8,128)S(1)}, f32[1,1,512,512]{3,2,1,0:T(8,128)}, u32[]{:S(2)}) copy-start(f32[1,1,512,512]{3,2,1,0:T(8,128)} %param.4) | copy-start | bytes 3145732
